TPU v7x, 32 devices: a whole 2x2x4 slice. The times are simulated.
32 devices in a mesh: seq: 16 (over z, y, core), head: 2 (over x).
Axes of the slice: x: 2, y: 2, z: 4, core: 2. Of those that a mesh axis runs over, the one named last changes fastest.
Arguments:
- inputs: bfloat16 [2, 2048, 1024], P(None, 'seq'), may hold values from -6 to 6
- encoded: bfloat16 [2, 6144, 1024], P(None, 'seq'), may hold values from -6 to 6
- tgt_bounds: int32 [2, 3], replicated, may hold values from 1 to 2048, as said below
- src_bounds: int32 [2, 3], replicated, may hold values from 1 to 6144, as said below
- self_query: bfloat16 [1024, 1024], P(None, 'head'), may hold values from -0.1875 to 0.1875
- self_key: bfloat16 [1024, 1024], P(None, 'head'), may hold values from -0.1875 to 0.1875
- self_value: bfloat16 [1024, 1024], P(None, 'head'), may hold values from -0.1875 to 0.1875
- self_out: bfloat16 [1024, 1024], P('head'), may hold values from -1.5 to 1.5
- cross_query: bfloat16 [1024, 1024], P(None, 'head'), may hold values from -0.1875 to 0.1875
- cross_key: bfloat16 [1024, 1024], P(None, 'head'), may hold values from -0.1875 to 0.1875
- cross_value: bfloat16 [1024, 1024], P(None, 'head'), may hold values from -0.1875 to 0.1875
- cross_out: bfloat16 [1024, 1024], P('head'), may hold values from -2.5 to 2.5
- ffn_in: bfloat16 [1024, 4096], P(None, 'head'), may hold values from -0.1875 to 0.1875
- ffn_out: bfloat16 [4096, 1024], P('head'), may hold values from -0.09375 to 0.09375
- adapter_down: bfloat16 [1024, 512], P(None, 'head'), may hold values from -0.1875 to 0.1875
- adapter_up: bfloat16 [512, 1024], P('head'), may hold values from -0.0625 to 0.0625
- norm1_gain: float32 [1024], replicated, may hold values from 0.25 to 1.75
- norm1_bias: float32 [1024], replicated, may hold values from -3 to 3
- norm2_gain: float32 [1024], replicated, may hold values from 0.25 to 1.75
- norm2_bias: float32 [1024], replicated, may hold values from -3 to 3
- norm3_gain: float32 [1024], replicated, may hold values from 0.25 to 1.75
- norm3_bias: float32 [1024], replicated, may hold values from -3 to 3
- cotangent: bfloat16 [2, 2048, 1024], P(None, 'seq'), may hold values from -6 to 6
Outputs:
- output: float32 [2, 2048, 1024], P(None, 'seq')
- grad_inputs: float32 [2, 2048, 1024], P(None, 'seq')
- grad_encoded: float32 [2, 6144, 1024], P(None, 'seq')
- grad_self_query: float32 [1024, 1024], P('seq', 'head')
- grad_self_key: float32 [1024, 1024], P('seq', 'head')
- grad_self_value: float32 [1024, 1024], P('seq', 'head')
- grad_self_out: float32 [1024, 1024], P('head', 'seq')
- grad_cross_query: float32 [1024, 1024], P('seq', 'head')
- grad_cross_key: float32 [1024, 1024], P('seq', 'head')
- grad_cross_value: float32 [1024, 1024], P('seq', 'head')
- grad_cross_out: float32 [1024, 1024], P('head', 'seq')
- grad_adapter_down: float32 [1024, 512], P(None, 'head')
- grad_adapter_up: float32 [512, 1024], P('head')
- grad_norm1_gain: float32 [1024], replicated
- grad_norm1_bias: float32 [1024], replicated
- grad_norm2_gain: float32 [1024], replicated
- grad_norm2_bias: float32 [1024], replicated
- grad_norm3_gain: float32 [1024], replicated
- grad_norm3_bias: float32 [1024], replicated
Inputs may be any that keep to these rules, and one draw needn't show every extreme that they name: `tgt_bounds`: each row is non-decreasing. In one packed sequence, chosen anew with each draw and the same one as in src_bounds, the first entry lies within the first 128 positions, the second within the last 128, and every further entry equals 2048, so that the sequence holds three documents; in every other sequence entry k (counted from 1) lies within 128 of 4 * k * 128. `src_bounds`: each row is non-decreasing. In the packed sequence chosen for tgt_bounds, the first entry lies within the first 384 positions, the second within the last 384, and every further entry equals 6144; in every other sequence entry k (counted from 1) lies within 384 of 4 * k * 384.
All inputs are finite; a program needn't handle non-finite values.
Results may differ from a plain program's by a relative error of at most 0.04.
Values may be sent and summed in bfloat16 or wider, within the bound.
No kernel may reach another device: no remote copies, remote signals or barrier semaphores. Data moves between devices by JAX's collectives and lax.ppermute only.
A program may use at most 320 MiB of HBM per device.

v0:
```python
import jax
import jax.numpy as jnp
from jax import lax
from jax.sharding import PartitionSpec as P

HEAD_DIM = 64


NEGATIVE = -1e30


def matrix_product(left, right):
    return jnp.dot(left, right, preferred_element_type=jnp.float32)


def times_transposed(left, right):
    return lax.dot_general(
        left, right, (((1,), (1,)), ((), ())), preferred_element_type=jnp.float32
    )


def transposed_times(left, right):
    return lax.dot_general(
        left, right, (((0,), (0,)), ((), ())), preferred_element_type=jnp.float32
    )


def norm_rows(values, norm_gain, norm_bias):
    average = jnp.mean(values, axis=-1, keepdims=True)
    centred = values - average
    spread = jnp.mean(centred * centred, axis=-1, keepdims=True)
    return centred * lax.rsqrt(spread + 1e-05) * norm_gain + norm_bias


def doc_ids(places, bounds):
    return jnp.sum((places[None, :, None] >= bounds[:, None, :]).astype(jnp.int32), axis=2)


def block_length(row_count):
    for candidate in (1024, 512, 256, 128):
        return candidate
    return row_count


def allowed_pairs(query_places, query_docs, key_places, bounds, causal):
    allowed = query_docs[:, :, None] == doc_ids(key_places, bounds)[:, None, :]
    if causal:
        allowed = jnp.logical_and(allowed, (query_places[:, None] >= key_places[None, :])[None])
    return allowed


def fold_keys(running, key_rows, value_rows, first_row, setting):
    queries, query_places, query_docs, bounds, causal = setting
    pack_count, row_count = (key_rows.shape[0], key_rows.shape[1])
    heads_here = queries.shape[2]
    key_heads = key_rows.reshape(pack_count, row_count, heads_here, HEAD_DIM)
    value_heads = value_rows.reshape(pack_count, row_count, heads_here, HEAD_DIM)
    key_places = first_row + jnp.arange(row_count, dtype=jnp.int32)
    allowed = allowed_pairs(query_places, query_docs, key_places, bounds, causal)[:, :, None, :]

    def fold_compute(state):
        highest, denominator, summed = state
        scores = jnp.einsum(
            "pqhd,pkhd->pqhk", queries, key_heads, preferred_element_type=jnp.float32
        ) * HEAD_DIM ** (-0.5)
        scores = jnp.where(allowed, scores, NEGATIVE)
        new_highest = jnp.maximum(highest, jnp.max(scores, axis=3))
        weights = jnp.where(allowed, jnp.exp(scores - new_highest[:, :, :, None]), 0.0)
        fading = jnp.exp(highest - new_highest)
        denominator = denominator * fading + jnp.sum(weights, axis=3)
        summed = summed * fading[:, :, :, None] + jnp.einsum(
            "pqhk,pkhd->pqhd",
            weights.astype(jnp.bfloat16),
            value_heads,
            preferred_element_type=jnp.float32,
        )
        return (new_highest, denominator, summed)

    def unchanged(state):
        return state

    return lax.cond(jnp.any(allowed), fold_compute, unchanged, running)


def fold_piece(running, key_rows, value_rows, setting):
    row_count = key_rows.shape[1]
    length = block_length(row_count)

    def fold_block_step(carried, number):
        offset = number * length
        key_block = lax.dynamic_slice_in_dim(key_rows, offset, length, 1)
        value_block = lax.dynamic_slice_in_dim(value_rows, offset, length, 1)
        return (fold_keys(carried, key_block, value_block, offset, setting), None)

    running, unused = lax.scan(
        fold_block_step, running, jnp.arange(row_count // length, dtype=jnp.int32)
    )
    return running


def finish(running):
    highest, denominator, summed = running
    attended = summed / denominator[:, :, :, None]
    return (attended, highest + jnp.log(denominator))


def attention_back(setting, key_rows, value_rows, first_row, attended, grad_heads, log_total):
    queries, query_places, query_docs, bounds, causal = setting
    pack_count, row_count = (key_rows.shape[0], key_rows.shape[1])
    heads_here = queries.shape[2]
    width = heads_here * HEAD_DIM
    length = block_length(row_count)
    scaling = HEAD_DIM ** (-0.5)
    balance = jnp.sum(grad_heads.astype(jnp.float32) * attended, axis=3)

    def attention_block_step(grad_query, number):
        offset = number * length
        key_block = lax.dynamic_slice_in_dim(key_rows, offset, length, 1).reshape(
            pack_count, length, heads_here, HEAD_DIM
        )
        value_block = lax.dynamic_slice_in_dim(value_rows, offset, length, 1).reshape(
            pack_count, length, heads_here, HEAD_DIM
        )
        key_places = first_row + offset + jnp.arange(length, dtype=jnp.int32)
        allowed = allowed_pairs(query_places, query_docs, key_places, bounds, causal)[:, :, None, :]

        def block_compute(grad_query):
            scores = (
                jnp.einsum(
                    "pqhd,pkhd->pqhk", queries, key_block, preferred_element_type=jnp.float32
                )
                * scaling
            )
            probability = jnp.where(allowed, jnp.exp(scores - log_total[:, :, :, None]), 0.0)
            grad_prob = jnp.einsum(
                "pqhd,pkhd->pqhk", grad_heads, value_block, preferred_element_type=jnp.float32
            )
            grad_score = (probability * (grad_prob - balance[:, :, :, None])).astype(jnp.bfloat16)
            grad_query = (
                grad_query
                + jnp.einsum(
                    "pqhk,pkhd->pqhd", grad_score, key_block, preferred_element_type=jnp.float32
                )
                * scaling
            )
            grad_key = (
                jnp.einsum(
                    "pqhk,pqhd->pkhd", grad_score, queries, preferred_element_type=jnp.float32
                )
                * scaling
            )
            grad_value = jnp.einsum(
                "pqhk,pqhd->pkhd",
                probability.astype(jnp.bfloat16),
                grad_heads,
                preferred_element_type=jnp.float32,
            )
            return (
                grad_query,
                (
                    grad_key.reshape(pack_count, length, width),
                    grad_value.reshape(pack_count, length, width),
                ),
            )

        def skipped(grad_query):
            nothing = jnp.zeros((pack_count, length, width), jnp.float32)
            return (grad_query, (nothing, nothing))

        return lax.cond(jnp.any(allowed), block_compute, skipped, grad_query)

    grad_query, key_terms = lax.scan(
        attention_block_step,
        jnp.zeros(queries.shape, jnp.float32),
        jnp.arange(row_count // length, dtype=jnp.int32),
    )
    grad_keys = jnp.moveaxis(key_terms[0], 0, 1).reshape(pack_count, row_count, width)
    grad_values = jnp.moveaxis(key_terms[1], 0, 1).reshape(pack_count, row_count, width)
    return (grad_query, grad_keys, grad_values)


def on_device(
    inputs,
    encoded,
    tgt_bounds,
    src_bounds,
    self_query,
    self_key,
    self_value,
    self_out,
    cross_query,
    cross_key,
    cross_value,
    cross_out,
    ffn_in,
    ffn_out,
    adapter_down,
    adapter_up,
    norm1_gain,
    norm1_bias,
    norm2_gain,
    norm2_bias,
    norm3_gain,
    norm3_bias,
    cotangent,
):
    pack_count, row_count, model_width = inputs.shape
    source_rows = encoded.shape[1]
    local_width = self_query.shape[1]
    heads_here = local_width // HEAD_DIM
    position = lax.axis_index("seq")
    query_places = position * row_count + jnp.arange(row_count, dtype=jnp.int32)
    query_docs = doc_ids(query_places, tgt_bounds)
    flat_inputs = inputs.reshape(pack_count * row_count, model_width)
    flat_encoded = encoded.reshape(pack_count * source_rows, model_width)

    def heads_of(values, rows):
        return values.reshape(pack_count, rows, heads_here, HEAD_DIM)

    def empty_state():
        return (
            jnp.full((pack_count, row_count, heads_here), NEGATIVE, jnp.float32),
            jnp.zeros((pack_count, row_count, heads_here), jnp.float32),
            jnp.zeros((pack_count, row_count, heads_here, HEAD_DIM), jnp.float32),
        )

    query_self = matrix_product(flat_inputs, self_query).astype(jnp.bfloat16)
    key_self = (
        matrix_product(flat_inputs, self_key)
        .astype(jnp.bfloat16)
        .reshape(pack_count, row_count, local_width)
    )
    value_self = (
        matrix_product(flat_inputs, self_value)
        .astype(jnp.bfloat16)
        .reshape(pack_count, row_count, local_width)
    )
    self_setting = (heads_of(query_self, row_count), query_places, query_docs, tgt_bounds, True)
    piece = (
        lax.all_gather(key_self, "seq", axis=1, tiled=True),
        lax.all_gather(value_self, "seq", axis=1, tiled=True),
    )
    self_state = fold_piece(empty_state(), piece[0], piece[1], self_setting)
    attended_self, log_self = finish(self_state)
    mixed_self = attended_self.reshape(pack_count * row_count, local_width).astype(jnp.bfloat16)
    out_self = lax.psum(matrix_product(mixed_self, self_out), "head")
    normed_one, norm_one_back = jax.vjp(
        norm_rows, flat_inputs.astype(jnp.float32) + out_self, norm1_gain, norm1_bias
    )
    normed_one_low = normed_one.astype(jnp.bfloat16)
    query_cross = matrix_product(normed_one_low, cross_query).astype(jnp.bfloat16)
    key_cross = (
        matrix_product(flat_encoded, cross_key)
        .astype(jnp.bfloat16)
        .reshape(pack_count, source_rows, local_width)
    )
    value_cross = (
        matrix_product(flat_encoded, cross_value)
        .astype(jnp.bfloat16)
        .reshape(pack_count, source_rows, local_width)
    )
    cross_setting = (heads_of(query_cross, row_count), query_places, query_docs, src_bounds, False)
    piece = (
        lax.all_gather(key_cross, "seq", axis=1, tiled=True),
        lax.all_gather(value_cross, "seq", axis=1, tiled=True),
    )
    cross_state = fold_piece(empty_state(), piece[0], piece[1], cross_setting)
    attended_cross, log_cross = finish(cross_state)
    mixed_cross = attended_cross.reshape(pack_count * row_count, local_width).astype(jnp.bfloat16)
    out_cross = lax.psum(matrix_product(mixed_cross, cross_out), "head")
    normed_two, norm_two_back = jax.vjp(norm_rows, normed_one + out_cross, norm2_gain, norm2_bias)
    normed_two_low = normed_two.astype(jnp.bfloat16)
    hidden = matrix_product(normed_two_low, ffn_in)
    activated, gelu_hidden_back = jax.vjp(jax.nn.gelu, hidden)
    activated_low = activated.astype(jnp.bfloat16)
    narrow = matrix_product(normed_two_low, adapter_down)
    narrow_act, gelu_narrow_back = jax.vjp(jax.nn.gelu, narrow)
    narrow_low = narrow_act.astype(jnp.bfloat16)
    branch_part = matrix_product(activated_low, ffn_out) + 4.0 * matrix_product(
        narrow_low, adapter_up
    )
    branch = lax.psum(branch_part, "head")
    normed_three, norm_three_back = jax.vjp(norm_rows, normed_two + branch, norm3_gain, norm3_bias)
    grad_third, grad_gain_three, grad_bias_three = norm_three_back(
        cotangent.reshape(pack_count * row_count, model_width).astype(jnp.float32)
    )
    grad_branch = grad_third.astype(jnp.bfloat16)
    grad_hidden = gelu_hidden_back(times_transposed(grad_branch, ffn_out))[0].astype(jnp.bfloat16)
    grad_narrow = gelu_narrow_back(4.0 * times_transposed(grad_branch, adapter_up))[0].astype(
        jnp.bfloat16
    )
    grad_adapter_up = 4.0 * transposed_times(narrow_low, grad_branch)
    grad_adapter_down = transposed_times(normed_two_low, grad_narrow)
    grad_two_part = times_transposed(grad_hidden, ffn_in) + times_transposed(
        grad_narrow, adapter_down
    )
    grad_two = grad_third + lax.psum(grad_two_part, "head")
    grad_second, grad_gain_two, grad_bias_two = norm_two_back(grad_two)
    grad_second_low = grad_second.astype(jnp.bfloat16)
    grad_cross_out = transposed_times(mixed_cross, grad_second_low)
    grad_mixed_cross = heads_of(
        times_transposed(grad_second_low, cross_out).astype(jnp.bfloat16), row_count
    )
    key_cross_all, value_cross_all, key_self_all, value_self_all = (
        lax.all_gather(key_cross, "seq", axis=1, tiled=True),
        lax.all_gather(value_cross, "seq", axis=1, tiled=True),
        lax.all_gather(key_self, "seq", axis=1, tiled=True),
        lax.all_gather(value_self, "seq", axis=1, tiled=True),
    )
    grad_query_cross, grad_keys_cross, grad_values_cross = attention_back(
        cross_setting,
        key_cross_all,
        value_cross_all,
        0,
        attended_cross,
        grad_mixed_cross,
        log_cross,
    )
    grad_key_cross, grad_value_cross = (
        lax.psum_scatter(grad_keys_cross, "seq", scatter_dimension=1, tiled=True),
        lax.psum_scatter(grad_values_cross, "seq", scatter_dimension=1, tiled=True),
    )
    grad_query_cross = grad_query_cross.reshape(pack_count * row_count, local_width).astype(
        jnp.bfloat16
    )
    grad_key_cross = grad_key_cross.reshape(pack_count * source_rows, local_width).astype(
        jnp.bfloat16
    )
    grad_value_cross = grad_value_cross.reshape(pack_count * source_rows, local_width).astype(
        jnp.bfloat16
    )
    grad_one_part = times_transposed(grad_query_cross, cross_query)
    grad_source_part = times_transposed(grad_key_cross, cross_key) + times_transposed(
        grad_value_cross, cross_value
    )
    grad_one_sum, grad_source = lax.psum((grad_one_part, grad_source_part), "head")
    grad_cross_query = transposed_times(normed_one_low, grad_query_cross)
    grad_cross_key = transposed_times(flat_encoded, grad_key_cross)
    grad_cross_value = transposed_times(flat_encoded, grad_value_cross)
    grad_first, grad_gain_one, grad_bias_one = norm_one_back(grad_second + grad_one_sum)
    grad_first_low = grad_first.astype(jnp.bfloat16)
    grad_self_out = transposed_times(mixed_self, grad_first_low)
    grad_mixed_self = heads_of(
        times_transposed(grad_first_low, self_out).astype(jnp.bfloat16), row_count
    )
    grad_query_self, grad_keys_self, grad_values_self = attention_back(
        self_setting, key_self_all, value_self_all, 0, attended_self, grad_mixed_self, log_self
    )
    grad_key_self, grad_value_self = (
        lax.psum_scatter(grad_keys_self, "seq", scatter_dimension=1, tiled=True),
        lax.psum_scatter(grad_values_self, "seq", scatter_dimension=1, tiled=True),
    )
    grad_query_self = grad_query_self.reshape(pack_count * row_count, local_width).astype(
        jnp.bfloat16
    )
    grad_key_self = grad_key_self.reshape(pack_count * row_count, local_width).astype(jnp.bfloat16)
    grad_value_self = grad_value_self.reshape(pack_count * row_count, local_width).astype(
        jnp.bfloat16
    )
    grad_in_part = (
        times_transposed(grad_query_self, self_query)
        + times_transposed(grad_key_self, self_key)
        + times_transposed(grad_value_self, self_value)
    )
    grad_inputs = grad_first + lax.psum(grad_in_part, "head")
    grad_self_query = transposed_times(flat_inputs, grad_query_self)
    grad_self_key = transposed_times(flat_inputs, grad_key_self)
    grad_self_value = transposed_times(flat_inputs, grad_value_self)
    weight_parts = (
        lax.psum_scatter(grad_self_query, "seq", scatter_dimension=0, tiled=True),
        lax.psum_scatter(grad_self_key, "seq", scatter_dimension=0, tiled=True),
        lax.psum_scatter(grad_self_value, "seq", scatter_dimension=0, tiled=True),
        lax.psum_scatter(grad_self_out, "seq", scatter_dimension=1, tiled=True),
        lax.psum_scatter(grad_cross_query, "seq", scatter_dimension=0, tiled=True),
        lax.psum_scatter(grad_cross_key, "seq", scatter_dimension=0, tiled=True),
        lax.psum_scatter(grad_cross_value, "seq", scatter_dimension=0, tiled=True),
        lax.psum_scatter(grad_cross_out, "seq", scatter_dimension=1, tiled=True),
    )
    small_parts = lax.psum(
        (
            grad_adapter_down,
            grad_adapter_up,
            grad_gain_one,
            grad_bias_one,
            grad_gain_two,
            grad_bias_two,
            grad_gain_three,
            grad_bias_three,
        ),
        "seq",
    )
    return (
        normed_three.reshape(pack_count, row_count, model_width),
        grad_inputs.reshape(pack_count, row_count, model_width),
        grad_source.reshape(pack_count, source_rows, model_width),
        weight_parts[0],
        weight_parts[1],
        weight_parts[2],
        weight_parts[3],
        weight_parts[4],
        weight_parts[5],
        weight_parts[6],
        weight_parts[7],
        small_parts[0],
        small_parts[1],
        small_parts[2],
        small_parts[3],
        small_parts[4],
        small_parts[5],
        small_parts[6],
        small_parts[7],
    )


def solution(mesh):
    placed = (
        P(None, "seq", None),
        P(None, "seq", None),
        P(),
        P(),
        P(None, "head"),
        P(None, "head"),
        P(None, "head"),
        P("head", None),
        P(None, "head"),
        P(None, "head"),
        P(None, "head"),
        P("head", None),
        P(None, "head"),
        P("head", None),
        P(None, "head"),
        P("head", None),
        P(),
        P(),
        P(),
        P(),
        P(),
        P(),
        P(None, "seq", None),
    )
    return jax.shard_map(
        on_device,
        mesh=mesh,
        in_specs=placed,
        out_specs=(
            P(None, "seq", None),
            P(None, "seq", None),
            P(None, "seq", None),
            P("seq", "head"),
            P("seq", "head"),
            P("seq", "head"),
            P("head", "seq"),
            P("seq", "head"),
            P("seq", "head"),
            P("seq", "head"),
            P("head", "seq"),
            P(None, "head"),
            P("head", None),
            P(),
            P(),
            P(),
            P(),
            P(),
            P(),
        ),
        check_vma=False,
    )
```

profile of v0, /device:TPU:0, one launch (start us, length us, event | category | flops | bytes accessed | tf_op | source)
XLA Modules:
  0.0 2478.0 jit_solution(1231674863412942728)
XLA Ops:
  14.2 52.6 %all-gather.5.cloned.1.call-done = bf16[2,2048,512]{1,2,0:T(8,128)(2,1)} async-done(((bf16[2,128,512]{1,2,0:T(8,128)(2,1)}), bf16[2,2048,512]{1,2,0:T(8,128)(2,1)}) %all-gather.5.cloned.1.call-update) | async-done | bytes 4194320 | tf_op jit(solution)/shard_map/all_gather | solution.py:240
  66.7 54.1 %all-gather.7.cloned.1.call-done = bf16[2,2048,512]{1,2,0:T(8,128)(2,1)} async-done(((bf16[2,128,512]{1,2,0:T(8,128)(2,1)}), bf16[2,2048,512]{1,2,0:T(8,128)(2,1)}) %all-gather.7.cloned.1.call-update) | async-done | bytes 4194320 | tf_op jit(solution)/shard_map/all_gather | solution.py:241
  200.8 100.9 %all-gather.11.cloned.1.call-done = bf16[2,6144,512]{1,2,0:T(8,128)(2,1)} async-done(((bf16[2,384,512]{1,2,0:T(8,128)(2,1)}), bf16[2,6144,512]{1,2,0:T(8,128)(2,1)}) %all-gather.11.cloned.1.call-update) | async-done | bytes 12582928 | tf_op jit(solution)/shard_map/all_gather | solution.py:265
  301.7 105.0 %all-gather.9.cloned.1.call-done = bf16[2,6144,512]{1,2,0:T(8,128)(2,1)} async-done(((bf16[2,384,512]{1,2,0:T(8,128)(2,1)}), bf16[2,6144,512]{1,2,0:T(8,128)(2,1)}) %all-gather.9.cloned.1.call-update) | async-done | bytes 12582928 | tf_op jit(solution)/shard_map/all_gather | solution.py:264
  407.6 90.9 %while.64 = (s32[]{:T(128)}, f32[2,128,8]{1,2,0:T(8,128)S(1)}, f32[2,128,8]{1,2,0:T(8,128)S(1)}, f32[2,128,8,64]{1,3,2,0:T(8,128)}, s32[2,128]{1,0:T(2,128)S(1)}...) while((s32[]{:T(128)}, f32[2,128,8]{1,2,0:T(8,128)S(1)}, ...), condition=%wide.region_19.20_spmd, body=%wide.region_12.19_spmd.sunk | while | flops 564941824 | bytes 44459392 | solution.py:95
  550.8 40.2 %all-reduce.15.cloned.1.call-done = f32[256,1024]{1,0:T(8,128)} async-done(((f32[256,1024]{1,0:T(8,128)}), f32[256,1024]{1,0:T(8,128)}) %all-reduce.15.cloned.1.call-update) | async-done | bytes 1048592 | tf_op jit(solution)/shard_map/psum | solution.py:282
  610.0 40.1 %all-reduce.17.cloned.1.call-done = f32[256,1024]{1,0:T(8,128)} async-done(((f32[256,1024]{1,0:T(8,128)}), f32[256,1024]{1,0:T(8,128)}) %all-reduce.17.cloned.1.call-update) | async-done | bytes 1048592 | tf_op jit(solution)/shard_map/psum | solution.py:297
  655.5 234.6 %while.65 = (s32[]{:T(128)}, f32[2,128,8,64]{1,3,2,0:T(8,128)S(1)}, f32[6,2,1024,512]{3,2,0,1:T(8,128)}, f32[6,2,1024,512]{3,2,0,1:T(8,128)}, s32[2,128]{1,0:T(2...) while((s32[]{:T(128)}, f32[2,128,8,64]{1,3,2,0:T(8,128)S(1)}, ...), condition=%wide.region_37.38_spmd, body=%wide.region_32.37_spmd.sunk | while | flops 1365001216 | bytes 97306448 | solution.py:172
  894.0 40.1 %all-reduce.19.cloned.1.call-done = f32[256,1024]{1,0:T(8,128)} async-done(((f32[256,1024]{1,0:T(8,128)}), f32[256,1024]{1,0:T(8,128)}) %all-reduce.19.cloned.1.call-update) | async-done | bytes 1048592 | tf_op jit(solution)/shard_map/psum | solution.py:336
  939.5 66.5 %while.67 = (s32[]{:T(128)}, f32[2,128,8,64]{1,3,2,0:T(8,128)S(1)}, f32[2,2,1024,512]{3,2,0,1:T(8,128)}, f32[2,2,1024,512]{3,2,0,1:T(8,128)}, s32[2,128]{1,0:T(2...) while((s32[]{:T(128)}, f32[2,128,8,64]{1,3,2,0:T(8,128)S(1)}, ...), condition=%wide.region_47.48_spmd.clone, body=%wide.region_42.47_spmd.clone.sunk | while | flops 1365394560 | bytes 97573720 | solution.py:172
  1012.0 111.0 %reduce-scatter.23.cloned.1.call-done = f32[2,128,512]{2,1,0:T(8,128)} async-done(((f32[2,2048,512]{2,1,0:T(8,128)}), f32[2,128,512]{2,1,0:T(8,128)}) %reduce-scatter.23.cloned.1.call-update) | async-done | bytes 524304 | tf_op jit(solution)/shard_map/reduce_scatter | solution.py:350
  1124.2 107.9 %reduce-scatter.25.cloned.1.call-done = f32[2,128,512]{2,1,0:T(8,128)} async-done(((f32[2,2048,512]{2,1,0:T(8,128)}), f32[2,128,512]{2,1,0:T(8,128)}) %reduce-scatter.25.cloned.1.call-update) | async-done | bytes 524304 | tf_op jit(solution)/shard_map/reduce_scatter | solution.py:351
  1236.8 243.5 %reduce-scatter.27.cloned.1.call-done = f32[2,384,512]{2,1,0:T(8,128)} async-done(((f32[2,6144,512]{2,1,0:T(8,128)}), f32[2,384,512]{2,1,0:T(8,128)}) %reduce-scatter.27.cloned.1.call-update) | async-done | bytes 1572880 | tf_op jit(solution)/shard_map/reduce_scatter | solution.py:320
  1485.7 242.3 %reduce-scatter.29.cloned.1.call-done = f32[2,384,512]{2,1,0:T(8,128)} async-done(((f32[2,6144,512]{2,1,0:T(8,128)}), f32[2,384,512]{2,1,0:T(8,128)}) %reduce-scatter.29.cloned.1.call-update) | async-done | bytes 1572880 | tf_op jit(solution)/shard_map/reduce_scatter | solution.py:321
  1774.8 59.2 %all-reduce = (f32[1024]{0:T(1024)}, f32[1024]{0:T(1024)}, f32[1024]{0:T(1024)}, f32[1024]{0:T(1024)}, f32[1024]{0:T(1024)}, /*index=5*/f32[1024]{0:T(1024)}) all-reduce(f32[1024]{0:T(1024)S(1)} %copy-done.79, f32[1024]{0:T(1024)S(1)} %copy-done.80, f32[1024]{0:T(1024)S(1)} %copy-done.77, ...), channel_id=1, replica_groups=mesh['seq'=16,'head'=2] {'seq'}, use_global_device_ids=true, to_apply=%region_65.66 | all-reduce | flops 6144 | bytes 49152 | tf_op jit(solution)/shard_map/psum | solution.py:379
  1845.2 99.1 %all-reduce.21.cloned.1.call-done = (f32[1024,256]{1,0:T(8,128)}, f32[256,1024]{1,0:T(8,128)}) async-done(((f32[1024,256]{1,0:T(8,128)}, f32[256,1024]{1,0:T(8,128)}), (f32[1024,256]{1,0:T(8,128)}, f32[256,1024]{1,0:T(8,128)})) %all-reduce.21.cloned.1.call-update) | async-done | bytes 2097168 | tf_op jit(solution)/shard_map/psum | solution.py:379
  1944.3 65.7 %reduce-scatter.35.cloned.1.call-done = f32[512,64]{0,1:T(8,128)} async-done(((f32[512,1024]{0,1:T(8,128)}), f32[512,64]{0,1:T(8,128)}) %reduce-scatter.35.cloned.1.call-update) | async-done | bytes 131088 | tf_op jit(solution)/shard_map/reduce_scatter | solution.py:377
  2010.0 64.7 %reduce-scatter.33.cloned.1.call-done = f32[64,512]{1,0:T(8,128)} async-done(((f32[1024,512]{1,0:T(8,128)}), f32[64,512]{1,0:T(8,128)}) %reduce-scatter.33.cloned.1.call-update) | async-done | bytes 131088 | tf_op jit(solution)/shard_map/reduce_scatter | solution.py:374
  2074.8 65.2 %reduce-scatter.31.cloned.1.call-done = f32[512,64]{0,1:T(8,128)} async-done(((f32[512,1024]{0,1:T(8,128)}), f32[512,64]{0,1:T(8,128)}) %reduce-scatter.31.cloned.1.call-update) | async-done | bytes 131088 | tf_op jit(solution)/shard_map/reduce_scatter | solution.py:373
  2140.0 64.9 %reduce-scatter.37.cloned.1.call-done = f32[64,512]{1,0:T(8,128)} async-done(((f32[1024,512]{1,0:T(8,128)}), f32[64,512]{1,0:T(8,128)}) %reduce-scatter.37.cloned.1.call-update) | async-done | bytes 131088
  2204.9 65.2 %reduce-scatter.39.cloned.1.call-done = f32[64,512]{1,0:T(8,128)} async-done(((f32[1024,512]{1,0:T(8,128)}), f32[64,512]{1,0:T(8,128)}) %reduce-scatter.39.cloned.1.call-update) | async-done | bytes 131088
  2270.0 64.9 %reduce-scatter.41.cloned.1.call-done = f32[64,512]{1,0:T(8,128)} async-done(((f32[1024,512]{1,0:T(8,128)}), f32[64,512]{1,0:T(8,128)}) %reduce-scatter.41.cloned.1.call-update) | async-done | bytes 131088
  2335.0 65.4 %reduce-scatter.43.cloned.1.call-done = f32[64,512]{1,0:T(8,128)} async-done(((f32[1024,512]{1,0:T(8,128)}), f32[64,512]{1,0:T(8,128)}) %reduce-scatter.43.cloned.1.call-update) | async-done | bytes 131088
  2400.3 64.9 %reduce-scatter.45.cloned.1.call-done = f32[64,512]{1,0:T(8,128)} async-done(((f32[1024,512]{1,0:T(8,128)}), f32[64,512]{1,0:T(8,128)}) %reduce-scatter.45.cloned.1.call-update) | async-done | bytes 131088
  (574 shorter events, 854.4 us)
Async XLA Ops:
  7.2 59.5 %all-gather.5.cloned.1.call-start = ((), (), s32[]{:S(2)}) async-start(), calls=%async_computation.12 | async-start | bytes 4456448 | tf_op jit(solution)/shard_map/all_gather | solution.py:240
  10.1 110.8 %all-gather.7.cloned.1.call-start = ((), (), s32[]{:S(2)}) async-start(), calls=%async_computation.13 | async-start | bytes 4456448 | tf_op jit(solution)/shard_map/all_gather | solution.py:241
  12.9 182.0 %all-reduce.11.cloned.1.call-start = ((), (), s32[]{:S(2)}) async-start(), calls=%async_computation.14 | async-start | bytes 2097152 | tf_op jit(solution)/shard_map/psum | solution.py:246
  144.5 157.2 %all-gather.11.cloned.1.call-start = ((), (), s32[]{:S(2)}) async-start(), calls=%async_computation.16 | async-start | bytes 13369344 | tf_op jit(solution)/shard_map/all_gather | solution.py:265
  150.2 256.5 %all-gather.9.cloned.1.call-start = ((), (), s32[]{:S(2)}) async-start(), calls=%async_computation.15 | async-start | bytes 13369344 | tf_op jit(solution)/shard_map/all_gather | solution.py:264
  154.9 387.2 %all-reduce.13.cloned.1.call-start = ((), (), s32[]{:S(2)}) async-start(), calls=%async_computation.17 | async-start | bytes 2097152 | tf_op jit(solution)/shard_map/psum | solution.py:270
  503.7 87.3 %all-reduce.15.cloned.1.call-start = ((), (), s32[]{:S(2)}) async-start(), calls=%async_computation.18 | async-start | bytes 2097152 | tf_op jit(solution)/shard_map/psum | solution.py:282
  550.7 99.4 %all-reduce.17.cloned.1.call-start = ((), (), s32[]{:S(2)}) async-start(), calls=%async_computation.19 | async-start | bytes 2097152 | tf_op jit(solution)/shard_map/psum | solution.py:297
  609.9 324.1 %all-reduce.19.cloned.1.call-start = ((), (), s32[]{:S(2)}) async-start(), calls=%async_computation.20 | async-start | bytes 2097152 | tf_op jit(solution)/shard_map/psum | solution.py:336
  893.9 229.2 %reduce-scatter.23.cloned.1.call-start = ((), (), s32[]{:S(2)}) async-start(), calls=%async_computation.21 | async-start | bytes 8912896 | tf_op jit(solution)/shard_map/reduce_scatter | solution.py:350
  1006.0 226.1 %reduce-scatter.25.cloned.1.call-start = ((), (), s32[]{:S(2)}) async-start(), calls=%async_computation.22 | async-start | bytes 8912896 | tf_op jit(solution)/shard_map/reduce_scatter | solution.py:351
  1006.7 473.5 %reduce-scatter.27.cloned.1.call-start = ((), (), s32[]{:S(2)}) async-start(), calls=%async_computation.23 | async-start | bytes 26738688 | tf_op jit(solution)/shard_map/reduce_scatter | solution.py:320
  1007.3 720.6 %reduce-scatter.29.cloned.1.call-start = ((), (), s32[]{:S(2)}) async-start(), calls=%async_computation.24 | async-start | bytes 26738688 | tf_op jit(solution)/shard_map/reduce_scatter | solution.py:321
  1008.1 834.7 %all-reduce.23.cloned.1.call-start = ((), (), s32[]{:S(2)}) async-start(), calls=%async_computation.34 | async-start | bytes 8388608 | tf_op jit(solution)/shard_map/psum | solution.py:365
  1735.3 209.0 %all-reduce.21.cloned.1.call-start = ((), (), s32[]{:S(2)}) async-start(), calls=%async_computation.33 | async-start | bytes 4194304 | tf_op jit(solution)/shard_map/psum | solution.py:379
  1739.2 270.9 %reduce-scatter.35.cloned.1.call-start = ((), (), s32[]{:S(2)}) async-start(), calls=%async_computation.27 | async-start | bytes 2228224 | tf_op jit(solution)/shard_map/reduce_scatter | solution.py:377
  1743.0 331.8 %reduce-scatter.33.cloned.1.call-start = ((), (), s32[]{:S(2)}) async-start(), calls=%async_computation.26 | async-start | bytes 2228224 | tf_op jit(solution)/shard_map/reduce_scatter | solution.py:374
  1746.0 394.0 %reduce-scatter.31.cloned.1.call-start = ((), (), s32[]{:S(2)}) async-start(), calls=%async_computation.25 | async-start | bytes 2228224 | tf_op jit(solution)/shard_map/reduce_scatter | solution.py:373
  1749.4 455.5 %reduce-scatter.37.cloned.1.call-start = ((), (), s32[]{:S(2)}) async-start(), calls=%async_computation.28 | async-start | bytes 2228224
  1754.2 515.9 %reduce-scatter.39.cloned.1.call-start = ((), (), s32[]{:S(2)}) async-start(), calls=%async_computation.29 | async-start | bytes 2228224
  1759.0 576.0 %reduce-scatter.41.cloned.1.call-start = ((), (), s32[]{:S(2)}) async-start(), calls=%async_computation.30 | async-start | bytes 2228224
  1763.8 636.6 %reduce-scatter.43.cloned.1.call-start = ((), (), s32[]{:S(2)}) async-start(), calls=%async_computation.31 | async-start | bytes 2228224
  1769.2 696.1 %reduce-scatter.45.cloned.1.call-start = ((), (), s32[]{:S(2)}) async-start(), calls=%async_computation.32 | async-start | bytes 2228224
  1944.3 525.0 %copy-start.49 = (f32[1024,256]{1,0:T(8,128)S(1)}, f32[1024,256]{1,0:T(8,128)}, u32[]{:S(2)}) copy-start(f32[1024,256]{1,0:T(8,128)} %get-tuple-element.1753) | copy-start | bytes 3145732
  (98 other events, 2797.4 us)
Sparse Core Ops, SparseCore 0:
  10.8 55.9 all-gather.4
  69.5 51.3 all-gather.6
  144.7 50.1 all-reduce.10
  197.7 103.9 all-gather.10
  304.6 102.1 all-gather.8
  503.8 38.2 all-reduce.12
  550.9 40.0 all-reduce.14
  610.1 40.0 all-reduce.16
  894.0 40.0 all-reduce.18
  1006.1 116.8 reduce-scatter.22
  1127.7 104.3 reduce-scatter.24
  1236.6 243.6 reduce-scatter.26
  1485.0 242.9 reduce-scatter.28
  1735.4 107.3 all-reduce.22
  1846.3 97.9 all-reduce.20
  1948.9 61.0 reduce-scatter.34
  2014.2 60.5 reduce-scatter.32
  2079.4 60.5 reduce-scatter.30
  2144.3 60.5 reduce-scatter.36
  2209.5 60.5 reduce-scatter.38
  2274.4 60.5 reduce-scatter.40
  2339.7 60.5 reduce-scatter.42
  2404.7 60.5 reduce-scatter.44
where the time goes:
time: 2490 us; the launch traced here: 2480 us
  waiting for transfers between devices  1850 us (74%)
  local copies, waits for them, and re-layouts  271 us (11%)
  matrix products  199 us (8%)
  other arithmetic  61.3 us (2%)
  blocking collectives  59.2 us (2%)
    unnamed x28, waiting for transfers between devices  328 us
    reduce_scatter x1, waiting for transfers between devices, on_device(): lax.psum_scatter(grad_keys_cross, 'seq', scatter_dimension=1, tiled=True)  244 us
    reduce_scatter x1, waiting for transfers between devices, on_device(): lax.psum_scatter(grad_values_cross, 'seq', scatter_dimension=1, tiled=True)  242 us
    dynamic_update_slice x24, local copies, waits for them, and re-layouts, attention_back(): lax.scan(attention_block_step, jnp.zeros(queries.shape, jnp.float32), jnp...  148 us
    reduce_scatter x1, waiting for transfers between devices, on_device(): lax.psum_scatter(grad_keys_self, 'seq', scatter_dimension=1, tiled=True)  111 us
    reduce_scatter x1, waiting for transfers between devices, on_device(): lax.psum_scatter(grad_values_self, 'seq', scatter_dimension=1, tiled=True)  108 us
    all_gather x1, waiting for transfers between devices, on_device(): lax.all_gather(key_cross, 'seq', axis=1, tiled=True)  105 us
    all_gather x1, waiting for transfers between devices, on_device(): lax.all_gather(value_cross, 'seq', axis=1, tiled=True)  101 us
  transfers between devices with their start and end apart: 23, of which 23 were waited for; matrix products, arithmetic and copies ran while one was open for 3% of the time, Pallas kernels for 0%

commit v1 on v0

v1 whole, which is shorter than its diff:
```python
import functools

import jax
import jax.numpy as jnp
from jax import lax
from jax.experimental import pallas as pl
from jax.experimental.pallas import tpu as pltpu
from jax.sharding import PartitionSpec as P

HEAD_DIM = 64
PAIR = 2 * HEAD_DIM
STATS = 16
LOWEST = -1e29
EXCLUDED = -1e30
F32 = jnp.float32
BF16 = jnp.bfloat16


def matrix_product(left, right):
    return jnp.dot(left, right, preferred_element_type=F32)


def contract(left, right, left_dim, right_dim):
    return lax.dot_general(
        left, right, (((left_dim,), (right_dim,)), ((), ())), preferred_element_type=F32
    )


def times_transposed(left, right):
    return contract(left, right, 1, 1)


def transposed_times(left, right):
    return contract(left, right, 0, 0)


def norm_rows(values, norm_gain, norm_bias):
    average = jnp.mean(values, axis=-1, keepdims=True)
    centred = values - average
    spread = jnp.mean(centred * centred, axis=-1, keepdims=True)
    return centred * lax.rsqrt(spread + 1e-05) * norm_gain + norm_bias


class Shape:
    def __init__(self, chips, groups, packs, rows, source_rows, starts, causal):
        self.chips, self.groups, self.packs, self.rows = chips, groups, packs, rows
        self.source_rows, self.starts, self.causal = source_rows, starts, causal
        self.step = groups
        while self.step > 1 and self.step * source_rows > 768:
            self.step //= 2
        self.steps = groups // self.step
        self.tile = 2 * rows
        self.length = 2 * chips * rows
        self.source_length = 2 * chips * source_rows


def position_range(shape, places, pack, target_bounds, source_bounds):
    starts = shape.starts
    low = jnp.zeros_like(places)
    high = jnp.zeros_like(places) + source_bounds[pack * starts]
    for entry in range(starts):
        later = places >= target_bounds[pack * starts + entry]
        low = jnp.where(later, source_bounds[pack * starts + entry], low)
        if entry + 1 < starts:
            following = source_bounds[pack * starts + entry + 1]
        else:
            following = jnp.int32(shape.source_length)
        high = jnp.where(later, following, high)
    if shape.causal:
        high = places + 1
    return low, high


def lane_places(shape, chip, core):
    lanes = lax.broadcasted_iota(jnp.int32, (1, shape.tile), 1)
    own = (2 * chip + core) * shape.rows + lanes
    other = (2 * chip + 1 - core) * shape.rows + lanes - shape.rows
    return jnp.where(lanes < shape.rows, own, other)


def step_conditions(shape, chip, pack, first_group, place, target_bounds, source_bounds):
    base, core = place[0], place[1]
    head = chip * (2 * shape.rows)
    tail = head + 2 * shape.rows - 1
    low_first, high_first = position_range(shape, head, pack, target_bounds, source_bounds)
    low_last, high_last = position_range(shape, tail, pack, target_bounds, source_bounds)
    begin = (base + 2 * first_group + core) * shape.source_rows
    end = begin + (2 * shape.step - 1) * shape.source_rows
    some = jnp.logical_and(low_first < end, high_last > begin)
    whole = jnp.logical_and(low_last <= begin, high_first >= end)
    return begin, some, whole


def source_places(shape, begin):
    size = shape.step * shape.source_rows
    rows = lax.broadcasted_iota(jnp.int32, (size, shape.tile), 0)
    places = begin + rows
    for group in range(1, shape.step):
        places = places + jnp.where(rows >= group * shape.source_rows, shape.source_rows, 0)
    return places


def both(own_ref, other_ref, chip, first, last, pack, rows):
    lanes = slice(pack * rows, (pack + 1) * rows)
    return jnp.concatenate(
        [own_ref[chip, first:last, lanes], other_ref[chip, first:last, lanes]], axis=1
    )


def one_head(pair_rows, head):
    feature = lax.broadcasted_iota(jnp.int32, pair_rows.shape, 0)
    mine = (feature >= HEAD_DIM) if head else (feature < HEAD_DIM)
    return jnp.where(mine, pair_rows, jnp.zeros_like(pair_rows))


def split_low(value):
    high = value.astype(BF16).astype(F32)
    return high, value - high


def split_parts(value):
    high = lax.reduce_precision(value, 8, 7)
    return high, value - high


def stat_rows(rows, width):
    index = lax.broadcasted_iota(jnp.int32, (STATS, width), 0)
    total = jnp.zeros((STATS, width), F32)
    for number, row in enumerate(rows):
        total = jnp.where(index == number, row, total)
    return total.astype(BF16)


def forward_kernel(
    shape, target_bounds, source_bounds, place, own_q, other_q, keys_values, own_out, other_out,
    value_t, maxima, sums, total,
):
    step_rows = shape.step * shape.source_rows
    for group in range(shape.groups):
        for pack in range(shape.packs):
            part = slice(pack * shape.source_rows, (pack + 1) * shape.source_rows)
            value_t[pack, :, group * shape.source_rows : (group + 1) * shape.source_rows] = (
                keys_values[group, 1, part, :].T
            )

    for pack in range(shape.packs):
        part = slice(pack * shape.source_rows, (pack + 1) * shape.source_rows)

        def per_chip(chip, unused, pack=pack, part=part):
            query = both(own_q, other_q, chip, 0, PAIR, pack, shape.rows)
            low, high = position_range(
                shape, lane_places(shape, chip, place[1]), pack, target_bounds, source_bounds
            )
            maxima[...] = jnp.full_like(maxima, LOWEST)
            sums[...] = jnp.zeros_like(sums)
            total[...] = jnp.zeros_like(total)
            for step in range(shape.steps):
                groups = slice(step * shape.step, (step + 1) * shape.step)
                begin, some, whole = step_conditions(
                    shape, chip, pack, step * shape.step, place, target_bounds, source_bounds
                )

                def fold(masked, step=step, groups=groups, begin=begin):
                    key_rows = keys_values[groups, 0, part, :].reshape(step_rows, PAIR)
                    if masked:
                        places = source_places(shape, begin)
                        allowed = jnp.logical_and(places >= low, places < high)
                    for head in range(2):
                        features = slice(head * HEAD_DIM, (head + 1) * HEAD_DIM)
                        scores = matrix_product(key_rows, one_head(query, head))
                        if masked:
                            scores = jnp.where(allowed, scores, EXCLUDED)
                        before = maxima[head : head + 1, :]
                        now = jnp.maximum(before, jnp.max(scores, axis=0, keepdims=True))
                        weights = jnp.exp(scores - now)
                        fading = jnp.exp(before - now)
                        maxima[head : head + 1, :] = now
                        sums[head : head + 1, :] = sums[head : head + 1, :] * fading + jnp.sum(
                            weights, axis=0, keepdims=True
                        )
                        values = value_t[pack, features, step * step_rows : (step + 1) * step_rows]
                        total[features, :] = total[features, :] * fading + matrix_product(
                            values, weights.astype(BF16)
                        )

                pl.when(jnp.logical_and(some, whole))(functools.partial(fold, False))
                pl.when(jnp.logical_and(some, jnp.logical_not(whole)))(
                    functools.partial(fold, True)
                )
            statistics = []
            for head in range(2):
                features = slice(head * HEAD_DIM, (head + 1) * HEAD_DIM)
                divisor = jnp.maximum(sums[head : head + 1, :], 1e-37)
                filled = sums[head : head + 1, :] > 0.0
                logs = jnp.where(filled, maxima[head : head + 1, :] + jnp.log(divisor), LOWEST)
                statistics.extend(split_low(logs))
                result = (total[features, :] / divisor).astype(BF16)
                for ref, offset in ((own_out, 0), (other_out, shape.rows)):
                    ref[chip, features, pack * shape.rows : (pack + 1) * shape.rows] = result[
                        :, offset : offset + shape.rows
                    ]
            statistics = stat_rows(statistics, shape.tile)
            for ref, offset in ((own_out, 0), (other_out, shape.rows)):
                ref[chip, PAIR : PAIR + STATS, pack * shape.rows : (pack + 1) * shape.rows] = (
                    statistics[:, offset : offset + shape.rows]
                )
            return 0

        lax.fori_loop(0, shape.chips, per_chip, 0)


def backward_kernel(
    shape, target_bounds, source_bounds, place, own_q, other_q, own_g, other_g, keys_values,
    own_dq, other_dq, key_grads, key_t, grad_key, grad_value, grad_query,
):
    step_rows = shape.step * shape.source_rows
    grad_key[...] = jnp.zeros_like(grad_key)
    grad_value[...] = jnp.zeros_like(grad_value)
    for group in range(shape.groups):
        for pack in range(shape.packs):
            part = slice(pack * shape.source_rows, (pack + 1) * shape.source_rows)
            key_t[pack, :, group * shape.source_rows : (group + 1) * shape.source_rows] = (
                keys_values[group, 0, part, :].T
            )

    for pack in range(shape.packs):
        part = slice(pack * shape.source_rows, (pack + 1) * shape.source_rows)

        def per_chip(chip, unused, pack=pack, part=part):
            query = both(own_q, other_q, chip, 0, PAIR, pack, shape.rows)
            grads = both(own_g, other_g, chip, 0, PAIR, pack, shape.rows)
            statistics = both(own_g, other_g, chip, PAIR, PAIR + STATS, pack, shape.rows).astype(F32)
            low, high = position_range(
                shape, lane_places(shape, chip, place[1]), pack, target_bounds, source_bounds
            )
            grad_query[...] = jnp.zeros_like(grad_query)
            for step in range(shape.steps):
                groups = slice(step * shape.step, (step + 1) * shape.step)
                begin, some, whole = step_conditions(
                    shape, chip, pack, step * shape.step, place, target_bounds, source_bounds
                )

                def fold(masked, step=step, groups=groups, begin=begin):
                    key_rows = keys_values[groups, 0, part, :].reshape(step_rows, PAIR)
                    value_rows = keys_values[groups, 1, part, :].reshape(step_rows, PAIR)
                    if masked:
                        places = source_places(shape, begin)
                        allowed = jnp.logical_and(places >= low, places < high)
                    probs, diffs, queries, gradients = [], [], [], []
                    lanes = slice(step * step_rows, (step + 1) * step_rows)
                    for head in range(2):
                        features = slice(head * HEAD_DIM, (head + 1) * HEAD_DIM)
                        head_query, head_grad = one_head(query, head), one_head(grads, head)
                        logs = statistics[2 * head : 2 * head + 1] + statistics[2 * head + 1 : 2 * head + 2]
                        delta = statistics[2 * head + 4 : 2 * head + 5] + statistics[2 * head + 5 : 2 * head + 6]
                        scores = matrix_product(key_rows, head_query)
                        if masked:
                            scores = jnp.where(allowed, scores, EXCLUDED)
                        weights = jnp.exp(scores - logs)
                        change = matrix_product(value_rows, head_grad)
                        diff = (weights * (change - delta)).astype(BF16)
                        grad_query[features, :] += matrix_product(key_t[pack, features, lanes], diff)
                        probs.append(weights.astype(BF16))
                        diffs.append(diff)
                        queries.append(head_query)
                        gradients.append(head_grad)
                    grad_key[pack, lanes, :] += times_transposed(
                        jnp.concatenate(diffs, axis=1), jnp.concatenate(queries, axis=1)
                    )
                    grad_value[pack, lanes, :] += times_transposed(
                        jnp.concatenate(probs, axis=1), jnp.concatenate(gradients, axis=1)
                    )

                pl.when(jnp.logical_and(some, whole))(functools.partial(fold, False))
                pl.when(jnp.logical_and(some, jnp.logical_not(whole)))(
                    functools.partial(fold, True)
                )
            result = (grad_query[...] * HEAD_DIM**-0.5).astype(BF16)
            for ref, offset in ((own_dq, 0), (other_dq, shape.rows)):
                ref[chip, :, pack * shape.rows : (pack + 1) * shape.rows] = result[
                    :, offset : offset + shape.rows
                ]
            return 0

        lax.fori_loop(0, shape.chips, per_chip, 0)

    for group in range(shape.groups):
        for pack in range(shape.packs):
            part = slice(pack * shape.source_rows, (pack + 1) * shape.source_rows)
            lanes = slice(group * shape.source_rows, (group + 1) * shape.source_rows)
            key_grads[group, 0, part, :] = grad_key[pack, lanes, :].astype(BF16)
            key_grads[group, 1, part, :] = grad_value[pack, lanes, :].astype(BF16)


def smem():
    return pl.BlockSpec(memory_space=pltpu.SMEM)


def vmem():
    return pl.BlockSpec(memory_space=pltpu.VMEM)


PARAMS = dict(vmem_limit_bytes=48 * 1024 * 1024)


def attention_forward(shape, bounds, place, own_q, other_q, keys_values):
    width = shape.packs * shape.rows
    pairs = shape.packs * shape.length * shape.groups * shape.source_rows
    message = jax.ShapeDtypeStruct((shape.chips, PAIR + STATS, width), BF16)
    return pl.pallas_call(
        functools.partial(forward_kernel, shape),
        out_shape=(message, message),
        in_specs=[smem()] * 3 + [vmem()] * 3,
        out_specs=(vmem(), vmem()),
        scratch_shapes=[
            pltpu.VMEM((shape.packs, PAIR, shape.groups * shape.source_rows), BF16),
            pltpu.VMEM((8, shape.tile), F32),
            pltpu.VMEM((8, shape.tile), F32),
            pltpu.VMEM((PAIR, shape.tile), F32),
        ],
        compiler_params=pltpu.CompilerParams(**PARAMS),
        cost_estimate=pl.CostEstimate(
            flops=8 * pairs * HEAD_DIM, bytes_accessed=6 * 1024 * 1024, transcendentals=2 * pairs
        ),
    )(bounds[0], bounds[1], place, own_q, other_q, keys_values)


def attention_backward(shape, bounds, place, own_q, other_q, own_g, other_g, keys_values):
    width = shape.packs * shape.rows
    pairs = shape.packs * shape.length * shape.groups * shape.source_rows
    source = shape.groups * shape.source_rows
    message = jax.ShapeDtypeStruct((shape.chips, PAIR, width), BF16)
    return pl.pallas_call(
        functools.partial(backward_kernel, shape),
        out_shape=(message, message, jax.ShapeDtypeStruct(keys_values.shape, BF16)),
        in_specs=[smem()] * 3 + [vmem()] * 5,
        out_specs=(vmem(), vmem(), vmem()),
        scratch_shapes=[
            pltpu.VMEM((shape.packs, PAIR, source), BF16),
            pltpu.VMEM((shape.packs, source, PAIR), F32),
            pltpu.VMEM((shape.packs, source, PAIR), F32),
            pltpu.VMEM((PAIR, shape.tile), F32),
        ],
        compiler_params=pltpu.CompilerParams(**PARAMS),
        cost_estimate=pl.CostEstimate(
            flops=20 * pairs * HEAD_DIM, bytes_accessed=8 * 1024 * 1024, transcendentals=2 * pairs
        ),
    )(bounds[0], bounds[1], place, own_q, other_q, own_g, other_g, keys_values)


def on_device(
    seq_size,
    head_size,
    inputs,
    encoded,
    tgt_bounds,
    src_bounds,
    self_query,
    self_key,
    self_value,
    self_out,
    cross_query,
    cross_key,
    cross_value,
    cross_out,
    ffn_in,
    ffn_out,
    adapter_down,
    adapter_up,
    norm1_gain,
    norm1_bias,
    norm2_gain,
    norm2_bias,
    norm3_gain,
    norm3_bias,
    cotangent,
):
    pack_count, row_count, model_width = inputs.shape
    source_rows = encoded.shape[1]
    local_width = self_query.shape[1]
    pairs_here = local_width // PAIR
    chips = seq_size // 2
    copies = chips // pairs_here
    rows = pack_count * row_count
    starts = tgt_bounds.shape[1]
    position = lax.axis_index("seq")
    core = position % 2
    base = position // (2 * pairs_here) * (2 * pairs_here)
    place = jnp.stack([base, core]).astype(jnp.int32)
    self_bounds = (tgt_bounds.reshape(-1), tgt_bounds.reshape(-1))
    cross_bounds = (tgt_bounds.reshape(-1), src_bounds.reshape(-1))
    self_shape = Shape(chips, pairs_here, pack_count, row_count, row_count, starts, True)
    cross_shape = Shape(chips, pairs_here, pack_count, row_count, source_rows, starts, False)
    flat_inputs = inputs.reshape(rows, model_width)
    flat_encoded = encoded.reshape(pack_count * source_rows, model_width)

    all_chips = [[2 * chip + side for chip in range(chips)] for side in range(2)]
    near_chips = [
        [2 * (copy * pairs_here + pair) + side for pair in range(pairs_here)]
        for copy in range(copies)
        for side in range(2)
    ]

    def swap_core(value):
        return lax.ppermute(value, "seq", [(i, i ^ 1) for i in range(seq_size)])

    def to_all(value):
        return lax.all_to_all(value, "seq", 0, 0, axis_index_groups=all_chips, tiled=True)

    def to_near(value):
        if pairs_here == 1:
            return value
        return lax.all_to_all(value, "seq", 0, 0, axis_index_groups=near_chips, tiled=True)

    def head_sum(value):
        if head_size == 2:
            low = lax.reduce_precision(value, 8, 7)
            return low + lax.ppermute(low.astype(BF16), "head", [(0, 1), (1, 0)]).astype(F32)
        return lax.psum(value, "head")

    def spread_queries(features):
        message = features.reshape(pairs_here, -1, rows)
        own = to_all(jnp.tile(message, (copies, 1, 1)))
        return own, swap_core(own)

    def pair_rows(keys, values):
        def cut(value):
            return value.reshape(-1, pairs_here, PAIR).transpose(1, 0, 2)

        return jnp.stack([cut(keys), cut(values)], axis=1)

    def join_rows(message):
        return message.transpose(1, 2, 0, 3).reshape(2, -1, local_width)

    def logs_of(message):
        stats = message[:, PAIR : PAIR + 4, :].astype(F32)
        return stats[:, 0::2] + stats[:, 1::2]

    def weighted(parts, logs):
        highest = jnp.max(logs, axis=0)
        weights = jnp.exp(logs - highest)
        denominator = jnp.sum(weights, axis=0)
        shares = weights / denominator
        split = parts.reshape(parts.shape[:-2] + (2, HEAD_DIM, rows)).astype(F32)
        merged = jnp.sum(split * shares[:, :, :, None, :], axis=0)
        return merged, highest + jnp.log(denominator)

    def collect(own_part, other_part):
        met = swap_core(other_part)
        parts = jnp.stack([own_part, met])
        logs = jnp.stack([logs_of(own_part), logs_of(met)])
        merged, total = weighted(parts[:, :, :PAIR], logs)
        high, low = split_parts(total)
        statistics = jnp.stack([high, low], axis=2).reshape(chips, 4, rows)
        statistics = jnp.pad(statistics, ((0, 0), (0, STATS - 4), (0, 0)))
        message = jnp.concatenate(
            [merged.reshape(chips, PAIR, rows).astype(BF16), statistics.astype(BF16)], axis=1
        )
        back = to_all(message)
        logs = logs_of(back).reshape(copies, pairs_here, 2, rows)
        features = back[:, :PAIR].reshape(copies, pairs_here, PAIR, rows)
        merged, total = weighted(features, logs)
        return merged, total

    def spread_grads(grad_features, merged, total):
        split = grad_features.reshape(pairs_here, 2, HEAD_DIM, rows).astype(F32)
        delta = jnp.sum(split * merged, axis=2)
        statistics = jnp.concatenate(
            [
                jnp.stack(split_parts(total), axis=2).reshape(pairs_here, 4, rows),
                jnp.stack(split_parts(delta), axis=2).reshape(pairs_here, 4, rows),
                jnp.zeros((pairs_here, STATS - 8, rows), F32),
            ],
            axis=1,
        ).astype(BF16)
        message = jnp.concatenate([grad_features.reshape(pairs_here, PAIR, rows), statistics], axis=1)
        return spread_queries(message)

    def collect_query_grads(own_part, other_part):
        total = (own_part.astype(F32) + swap_core(other_part).astype(F32)).astype(BF16)
        back = to_all(total).reshape(copies, local_width, rows)
        return jnp.sum(back.astype(F32), axis=0).astype(BF16)

    scaling = HEAD_DIM**-0.5
    query_self = (contract(self_query, flat_inputs, 0, 1) * scaling).astype(BF16)
    key_self = matrix_product(flat_inputs, self_key).astype(BF16)
    value_self = matrix_product(flat_inputs, self_value).astype(BF16)
    self_q = spread_queries(query_self)
    self_kv = to_near(pair_rows(key_self, value_self))
    own_part, other_part = attention_forward(self_shape, self_bounds, place, *self_q, self_kv)
    attended_self, log_self = collect(own_part, other_part)
    mixed_self = attended_self.reshape(local_width, rows).astype(BF16)
    out_self = head_sum(transposed_times(mixed_self, self_out))
    normed_one, norm_one_back = jax.vjp(
        norm_rows, flat_inputs.astype(F32) + out_self, norm1_gain, norm1_bias
    )
    normed_one_low = normed_one.astype(BF16)
    query_cross = (contract(cross_query, normed_one_low, 0, 1) * scaling).astype(BF16)
    key_cross = matrix_product(flat_encoded, cross_key).astype(BF16)
    value_cross = matrix_product(flat_encoded, cross_value).astype(BF16)
    cross_kv = to_near(pair_rows(key_cross, value_cross))
    cross_q = spread_queries(query_cross)
    own_part, other_part = attention_forward(cross_shape, cross_bounds, place, *cross_q, cross_kv)
    attended_cross, log_cross = collect(own_part, other_part)
    mixed_cross = attended_cross.reshape(local_width, rows).astype(BF16)
    out_cross = head_sum(transposed_times(mixed_cross, cross_out))
    normed_two, norm_two_back = jax.vjp(norm_rows, normed_one + out_cross, norm2_gain, norm2_bias)
    normed_two_low = normed_two.astype(BF16)
    hidden = matrix_product(normed_two_low, ffn_in)
    activated, gelu_hidden_back = jax.vjp(jax.nn.gelu, hidden)
    activated_low = activated.astype(BF16)
    narrow = matrix_product(normed_two_low, adapter_down)
    narrow_act, gelu_narrow_back = jax.vjp(jax.nn.gelu, narrow)
    narrow_low = narrow_act.astype(BF16)
    branch_part = matrix_product(activated_low, ffn_out) + 4.0 * matrix_product(
        narrow_low, adapter_up
    )
    branch = head_sum(branch_part)
    normed_three, norm_three_back = jax.vjp(norm_rows, normed_two + branch, norm3_gain, norm3_bias)
    grad_third, grad_gain_three, grad_bias_three = norm_three_back(
        cotangent.reshape(rows, model_width).astype(F32)
    )
    grad_branch = grad_third.astype(BF16)
    grad_hidden = gelu_hidden_back(times_transposed(grad_branch, ffn_out))[0].astype(BF16)
    grad_narrow = gelu_narrow_back(4.0 * times_transposed(grad_branch, adapter_up))[0].astype(BF16)
    grad_adapter_up = 4.0 * transposed_times(narrow_low, grad_branch)
    grad_adapter_down_t = transposed_times(grad_narrow, normed_two_low)
    grad_two_part = times_transposed(grad_hidden, ffn_in) + times_transposed(
        grad_narrow, adapter_down
    )
    adapters = lax.psum(
        jnp.concatenate([grad_adapter_up, grad_adapter_down_t], axis=0).astype(BF16), "seq"
    ).astype(F32)
    grad_two = grad_third + head_sum(grad_two_part)
    grad_second, grad_gain_two, grad_bias_two = norm_two_back(grad_two)
    grad_second_low = grad_second.astype(BF16)
    grad_cross_out_t = contract(grad_second_low, mixed_cross, 0, 1)
    grad_mixed_cross = times_transposed(cross_out, grad_second_low).astype(BF16)
    cross_g = spread_grads(grad_mixed_cross, attended_cross, log_cross)
    own_part, other_part, cross_dkv = attention_backward(
        cross_shape, cross_bounds, place, *cross_q, *cross_g, cross_kv
    )
    grad_query_cross = collect_query_grads(own_part, other_part)
    grad_key_cross, grad_value_cross = join_rows(to_near(cross_dkv))
    grad_one_sum = head_sum(transposed_times(grad_query_cross, contract_t(cross_query)))
    grad_source = head_sum(
        times_transposed(grad_key_cross, cross_key) + times_transposed(grad_value_cross, cross_value)
    )
    grad_cross_query = contract(normed_one_low, grad_query_cross, 0, 1)
    grad_cross_key = transposed_times(flat_encoded, grad_key_cross)
    grad_cross_value = transposed_times(flat_encoded, grad_value_cross)
    grad_first, grad_gain_one, grad_bias_one = norm_one_back(grad_second + grad_one_sum)
    grad_first_low = grad_first.astype(BF16)
    grad_self_out_t = contract(grad_first_low, mixed_self, 0, 1)
    grad_mixed_self = times_transposed(self_out, grad_first_low).astype(BF16)
    self_g = spread_grads(grad_mixed_self, attended_self, log_self)
    own_part, other_part, self_dkv = attention_backward(
        self_shape, self_bounds, place, *self_q, *self_g, self_kv
    )
    grad_query_self = collect_query_grads(own_part, other_part)
    grad_key_self, grad_value_self = join_rows(to_near(self_dkv))
    grad_in_part = (
        transposed_times(grad_query_self, contract_t(self_query))
        + times_transposed(grad_key_self, self_key)
        + times_transposed(grad_value_self, self_value)
    )
    grad_inputs = grad_first + head_sum(grad_in_part)
    grad_self_query = contract(flat_inputs, grad_query_self, 0, 1)
    grad_self_key = transposed_times(flat_inputs, grad_key_self)
    grad_self_value = transposed_times(flat_inputs, grad_value_self)

    def scatter(parts):
        joined = jnp.concatenate([part.astype(BF16) for part in parts], axis=1)
        scattered = lax.psum_scatter(joined, "seq", scatter_dimension=0, tiled=True).astype(F32)
        return jnp.split(scattered, len(parts), axis=1)

    cross_out_t, cross_query_g, cross_key_g, cross_value_g = scatter(
        [grad_cross_out_t, grad_cross_query, grad_cross_key, grad_cross_value]
    )
    self_out_t, self_query_g, self_key_g, self_value_g = scatter(
        [grad_self_out_t, grad_self_query, grad_self_key, grad_self_value]
    )
    small = lax.psum(
        jnp.stack(
            [
                grad_gain_one,
                grad_bias_one,
                grad_gain_two,
                grad_bias_two,
                grad_gain_three,
                grad_bias_three,
            ]
        ),
        "seq",
    )
    half = adapter_up.shape[0]
    return (
        normed_three.reshape(pack_count, row_count, model_width),
        grad_inputs.reshape(pack_count, row_count, model_width),
        grad_source.reshape(pack_count, source_rows, model_width),
        self_query_g,
        self_key_g,
        self_value_g,
        self_out_t.T,
        cross_query_g,
        cross_key_g,
        cross_value_g,
        cross_out_t.T,
        adapters[half:].T,
        adapters[:half],
        small[0],
        small[1],
        small[2],
        small[3],
        small[4],
        small[5],
    )


def contract_t(weight):
    return weight.T


def solution(mesh):
    placed = (
        P(None, "seq", None),
        P(None, "seq", None),
        P(),
        P(),
        P(None, "head"),
        P(None, "head"),
        P(None, "head"),
        P("head", None),
        P(None, "head"),
        P(None, "head"),
        P(None, "head"),
        P("head", None),
        P(None, "head"),
        P("head", None),
        P(None, "head"),
        P("head", None),
        P(),
        P(),
        P(),
        P(),
        P(),
        P(),
        P(None, "seq", None),
    )
    return jax.shard_map(
        functools.partial(on_device, mesh.shape["seq"], mesh.shape["head"]),
        mesh=mesh,
        in_specs=placed,
        out_specs=(
            P(None, "seq", None),
            P(None, "seq", None),
            P(None, "seq", None),
            P("seq", "head"),
            P("seq", "head"),
            P("seq", "head"),
            P("head", "seq"),
            P("seq", "head"),
            P("seq", "head"),
            P("seq", "head"),
            P("head", "seq"),
            P(None, "head"),
            P("head", None),
            P(),
            P(),
            P(),
            P(),
            P(),
            P(),
        ),
        check_vma=False,
    )
```

time: 2490 us -> 628 us (0.25)
  waiting for transfers between devices: 1850 us -> 133 us
  local copies, waits for them, and re-layouts: 271 us -> 74 us
  matrix products: 199 us -> 55.4 us
  blocking collectives: 59.2 us -> 162 us
  Pallas kernels: 0 us -> 94.3 us
  starting transfers between devices: 1.75 us -> 46.3 us
    reduce_scatter x7 -> x0, waiting for transfers between devices: 900 us -> none  [the longest x1 244 us: on_device(): lax.psum_scatter(grad_keys_cross, 'seq', scatter_dimension=1, tiled=True)]
    all_gather x4 -> x0, waiting for transfers between devices: 313 us -> none  [the longest x1 105 us: on_device(): lax.all_gather(key_cross, 'seq', axis=1, tiled=True)]
    psum x7 -> x1, waiting for transfers between devices: 306 us -> 0.02 us  [on_device(): lax.psum(jnp.concatenate([grad_adapter_up, grad_adapter_down_t], axis=0)....]
    unnamed x28 -> x5, waiting for transfers between devices: 328 us -> 21.7 us
    dynamic_update_slice x24 -> x0, local copies, waits for them, and re-layouts: 148 us -> none  [attention_back(): lax.scan(attention_block_step, jnp.zeros(queries.shape, jnp.float32), jnp...]
    dot_general x82 -> x33, matrix products: 199 us -> 55.4 us  [the longest x25 43.6 us: contract(): lax.dot_general(left, right, (((left_dim,), (right_dim,)), ((), ())), pre...]
    all_to_all x0 -> x5, blocking collectives: none -> 102 us  [to_all(): lax.all_to_all(value, 'seq', 0, 0, axis_index_groups=all_chips, tiled=True)]
    pallas_call x0 -> x4, Pallas kernels: none -> 94.3 us  [the longest x2 50.3 us: attention_backward(): pl.pallas_call(functools.partial(backward_kernel, shape), out_shape=(mess...]
  transfers between devices with their start and end apart: 23 -> 25, of which waited for: 23 -> 18; matrix products, arithmetic and copies ran while one was open for 3% -> 17% of each run, Pallas kernels for 0% -> 3%
where the time goes in v1:
time: 628 us; the launch traced here: 620 us
  blocking collectives  162 us (26%)
  waiting for transfers between devices  133 us (21%)
  Pallas kernels  94.3 us (15%)
  local copies, waits for them, and re-layouts  74 us (12%)
  matrix products  55.4 us (9%)
  starting transfers between devices  46.3 us (7%)
  other arithmetic  39.6 us (6%)
  between operations  15.6 us (2%)
    all_to_all x5, blocking collectives, to_all(): lax.all_to_all(value, 'seq', 0, 0, axis_index_groups=all_chips, tiled=True)  102 us
    psum x1, blocking collectives, on_device(): lax.psum(jnp.stack([grad_gain_one, grad_bias_one, grad_gain_two, grad_bia...  59.8 us
    pallas_call x2, Pallas kernels, attention_backward(): pl.pallas_call(functools.partial(backward_kernel, shape), out_shape=(mess...  50.3 us
    pallas_call x2, Pallas kernels, attention_forward(): pl.pallas_call(functools.partial(forward_kernel, shape), out_shape=(messa...  44 us
    ppermute x7, waiting for transfers between devices, head_sum(): lax.ppermute(low.astype(BF16), 'head', [(0, 1), (1, 0)]).astype(F32)  43.9 us
    dot_general x25, matrix products, contract(): lax.dot_general(left, right, (((left_dim,), (right_dim,)), ((), ())), pre...  43.6 us
    unnamed x163, local copies, waits for them, and re-layouts  42.8 us
    all_to_all x4, waiting for transfers between devices, to_near(): lax.all_to_all(value, 'seq', 0, 0, axis_index_groups=near_chips, tiled=True)  40.2 us
  transfers between devices with their start and end apart: 25, of which 18 were waited for; matrix products, arithmetic and copies ran while one was open for 17% of the time, Pallas kernels for 3%

profile of v1, /device:TPU:0, one launch (start us, length us, event | category | flops | bytes accessed | tf_op | source)
XLA Modules:
  0.0 619.9 jit_solution(11163639360034832539)
XLA Ops:
  10.0 7.3 %all-to-all-start = ((bf16[8,128,256]{2,1,0:T(8,128)(2,1)}), bf16[8,128,256]{2,1,0:T(8,128)(2,1)S(1)}, u32[]{:S(2)}, u32[]{:S(2)}) async-start(bf16[8,128,256]{2,1,0:T(8,128)(2,1)} %bitcast.4), calls=%async_computation | async-start | bytes 1048576 | tf_op jit(solution)/shard_map/all_to_all | solution.py:408
  22.2 9.7 %all-to-all-done.own_q = bf16[8,128,256]{2,1,0:T(8,128)(2,1)S(1)} async-done(((bf16[8,128,256]{2,1,0:T(8,128)(2,1)}), bf16[8,128,256]{2,1,0:T(8,128)(2,1)S(1)}, u32[]{:S(2)}, u32[]{:S(2)}) %all-to-all-start) | async-done | bytes 524320 | tf_op jit(solution)/shard_map/all_to_all | solution.py:408
  35.6 6.9 %all-to-all-done.1.keys_values = bf16[4,2,256,128]{3,2,1,0:T(8,128)(2,1)S(1)} async-done(((bf16[4,2,256,128]{3,2,1,0:T(8,128)(2,1)}), bf16[4,2,256,128]{3,2,1,0:T(8,128)(2,1)S(1)}, u32[]{:S(2)}, u32[]{:S(2)}) %all-to-all-start.1) | async-done | bytes 524320 | tf_op jit(solution)/shard_map/all_to_all | solution.py:413
  44.4 14.5 %shard_map.366 = (bf16[8,144,256]{2,1,0:T(8,128)(2,1)S(1)}, bf16[8,144,256]{2,1,0:T(8,128)(2,1)}) custom-call(s32[6]{0:T(128)S(1)} %reshape.465.target_bounds.source_bounds, s32[6]{0:T(128)S(1)} %reshape.465.target_bounds.source_bounds, s32[2]{0:T(128)S(1)} %pad_add_fusion.place, bf16[8,128,256]{2,1,0:T(8,128)(2,1)S(1)} %all-to-all-done.own_q, ...), custom_call_target="tpu_custom_call" | custom-call | flops 1073741824 | bytes 6291456 | tf_op jit(solution)/shard_map/pallas_call | solution.py:310
  61.7 19.6 %all_to_all.60 = bf16[8,144,256]{2,1,0:T(8,128)(2,1)S(1)} all-to-all(bf16[8,144,256]{2,1,0:T(8,128)(2,1)S(1)} %fusion.41), channel_id=1, replica_groups={{0,4,8,12,16,20,24,28},{2,6,10,14,18,22,26,30},{1,5,9,13,17,21,25,29},{..., dimensions={0} | all-to-all | bytes 1179648 | tf_op jit(solution)/shard_map/all_to_all | solution.py:408
  85.6 10.9 %collective-permute-done.2 = bf16[256,1024]{1,0:T(8,128)(2,1)S(1)} collective-permute-done((bf16[256,1024]{1,0:T(8,128)(2,1)S(1)}, bf16[256,1024]{1,0:T(8,128)(2,1)S(1)}, u32[]{:S(2)}, u32[]{:S(2)}) %collective-permute-start.2) | collective-permute-done | bytes 524320 | tf_op jit(solution)/shard_map/ppermute | solution.py:418
  121.8 17.8 %all-to-all-done.4.keys_values = bf16[4,2,768,128]{3,2,1,0:T(8,128)(2,1)S(1)} async-done(((bf16[4,2,768,128]{3,2,1,0:T(8,128)(2,1)}), bf16[4,2,768,128]{3,2,1,0:T(8,128)(2,1)S(1)}, u32[]{:S(2)}, u32[]{:S(2)}) %all-to-all-start.4) | async-done | bytes 1572896 | tf_op jit(solution)/shard_map/all_to_all | solution.py:413
  141.1 29.5 %shard_map.367 = (bf16[8,144,256]{2,1,0:T(8,128)(2,1)S(1)}, bf16[8,144,256]{2,1,0:T(8,128)(2,1)}) custom-call(s32[6]{0:T(128)S(1)} %reshape.465.target_bounds.source_bounds, s32[6]{0:T(128)S(1)} %reshape.470.source_bounds, s32[2]{0:T(128)S(1)} %pad_add_fusion.place, bf16[8,128,256]{2,1,0:T(8,128)(2,1)S(1)} %copy-done.8, ...), custom_call_target="tpu_custom_call" | custom-call | flops 3221225472 | bytes 6291456 | tf_op jit(solution)/shard_map/pallas_call | solution.py:310
  175.2 22.6 %all_to_all.61 = bf16[8,144,256]{2,1,0:T(8,128)(2,1)S(1)} all-to-all(bf16[8,144,256]{2,1,0:T(8,128)(2,1)S(1)} %fusion.42), channel_id=1, replica_groups={{0,4,8,12,16,20,24,28},{2,6,10,14,18,22,26,30},{1,5,9,13,17,21,25,29},{..., dimensions={0} | all-to-all | bytes 1179648 | tf_op jit(solution)/shard_map/all_to_all | solution.py:408
  201.6 10.9 %collective-permute-done.5 = bf16[256,1024]{1,0:T(8,128)(2,1)S(1)} collective-permute-done((bf16[256,1024]{1,0:T(8,128)(2,1)S(1)}, bf16[256,1024]{1,0:T(8,128)(2,1)S(1)}, u32[]{:S(2)}, u32[]{:S(2)}) %collective-permute-start.5) | collective-permute-done | bytes 524320 | tf_op jit(solution)/shard_map/ppermute | solution.py:418
  221.1 9.9 %collective-permute-done.6 = bf16[256,1024]{1,0:T(8,128)(2,1)S(1)} collective-permute-done((bf16[256,1024]{1,0:T(8,128)(2,1)S(1)}, bf16[256,1024]{1,0:T(8,128)(2,1)S(1)}, u32[]{:S(2)}, u32[]{:S(2)}) %collective-permute-start.6) | collective-permute-done | bytes 524320 | tf_op jit(solution)/shard_map/ppermute | solution.py:418
  235.8 8.3 %fusion.37 = f32[256,1024]{1,0:T(8,128)} fusion(bf16[1024,2048]{1,0:T(8,128)(2,1)} %param.35, f32[256,2048]{1,0:T(8,128)} %copy-done.73, bf16[256,1024]{1,0:T(8,128)(2,1)} %add_convert_fusion.4, bf16[2048,1024]{1,0:T(8,128)(2,1)} %param.36), kind=kOutput, calls=%fused_computation.104 | convolution fusion | flops 2157969408 | bytes 12058624 | tf_op jit(solution)/shard_map/dot_general | solution.py:24
  249.8 8.4 %collective-permute-done.7 = bf16[256,1024]{1,0:T(8,128)(2,1)} collective-permute-done((bf16[256,1024]{1,0:T(8,128)(2,1)}, bf16[256,1024]{1,0:T(8,128)(2,1)}, u32[]{:S(2)}, u32[]{:S(2)}) %collective-permute-start.7) | collective-permute-done | bytes 524320 | tf_op jit(solution)/shard_map/ppermute | solution.py:418
  270.0 20.1 %all_to_all.62.own_g = bf16[8,144,256]{2,1,0:T(8,128)(2,1)S(1)} all-to-all(bf16[8,144,256]{2,1,0:T(8,128)(2,1)S(1)} %bitcast.234), channel_id=1, replica_groups={{0,4,8,12,16,20,24,28},{2,6,10,14,18,22,26,30},{1,5,9,13,17,21,25,29},{..., dimensions={0} | all-to-all | bytes 1179648 | tf_op jit(solution)/shard_map/all_to_all | solution.py:408
  292.0 33.9 %shard_map.368 = (bf16[8,128,256]{2,1,0:T(8,128)(2,1)S(1)}, bf16[8,128,256]{2,1,0:T(8,128)(2,1)S(1)}, bf16[4,2,768,128]{3,2,1,0:T(8,128)(2,1)}) custom-call(s32[6]{0:T(128)S(1)} %reshape.465.target_bounds.source_bounds, s32[6]{0:T(128)S(1)} %reshape.470.source_bounds, s32[2]{0:T(128)S(1)} %pad_add_fusion.place, bf16[8,128,256]{2,1,0:T(8,128)(2,1)S(1)} %copy-done.9, ...), custom_call_target="tpu_custom_call" | custom-call | flops 8053063680 | bytes 8388608 | tf_op jit(solution)/shard_map/pallas_call | solution.py:333
  330.1 19.5 %all_to_all.63 = bf16[8,128,256]{2,1,0:T(8,128)(2,1)} all-to-all(bf16[8,128,256]{2,1,0:T(8,128)(2,1)S(1)} %add_convert_fusion.1), channel_id=1, replica_groups={{0,4,8,12,16,20,24,28},{2,6,10,14,18,22,26,30},{1,5,9,13,17,21,25,29},{..., dimensions={0} | all-to-all | bytes 1048576 | tf_op jit(solution)/shard_map/all_to_all | solution.py:408
  367.1 8.3 %all-to-all-done.11 = bf16[4,2,768,128]{3,2,1,0:T(8,128)(2,1)} async-done(((bf16[4,2,768,128]{3,2,1,0:T(8,128)(2,1)}), bf16[4,2,768,128]{3,2,1,0:T(8,128)(2,1)}, u32[]{:S(2)}, u32[]{:S(2)}) %all-to-all-start.11) | async-done | bytes 1572896 | tf_op jit(solution)/shard_map/all_to_all | solution.py:413
  388.7 6.5 %copy.219 = bf16[1024,2048]{1,0:T(8,128)(2,1)} copy(bf16[1024,2048]{0,1:T(8,128)(2,1)} %pad_maximum_fusion.1) | data formatting | bytes 8388608
  403.3 20.6 %all_to_all.64.own_g = bf16[8,144,256]{2,1,0:T(8,128)(2,1)S(1)} all-to-all(bf16[8,144,256]{2,1,0:T(8,128)(2,1)S(1)} %bitcast.235), channel_id=1, replica_groups={{0,4,8,12,16,20,24,28},{2,6,10,14,18,22,26,30},{1,5,9,13,17,21,25,29},{..., dimensions={0} | all-to-all | bytes 1179648 | tf_op jit(solution)/shard_map/all_to_all | solution.py:408
  427.0 16.4 %shard_map.369 = (bf16[8,128,256]{2,1,0:T(8,128)(2,1)S(1)}, bf16[8,128,256]{2,1,0:T(8,128)(2,1)}, bf16[4,2,256,128]{3,2,1,0:T(8,128)(2,1)S(1)}) custom-call(s32[6]{0:T(128)S(1)} %reshape.465.target_bounds.source_bounds, s32[6]{0:T(128)S(1)} %reshape.465.target_bounds.source_bounds, s32[2]{0:T(128)S(1)} %pad_add_fusion.place, ...), custom_call_target="tpu_custom_call" | custom-call | flops 2684354560 | bytes 8388608 | tf_op jit(solution)/shard_map/pallas_call | solution.py:333
  450.7 7.1 %all-to-all-done.10 = bf16[4,2,256,128]{3,2,1,0:T(8,128)(2,1)} async-done(((bf16[4,2,256,128]{3,2,1,0:T(8,128)(2,1)}), bf16[4,2,256,128]{3,2,1,0:T(8,128)(2,1)}, u32[]{:S(2)}, u32[]{:S(2)}) %all-to-all-start.10) | async-done | bytes 524320 | tf_op jit(solution)/shard_map/all_to_all | solution.py:413
  481.7 6.7 %copy.217 = bf16[1024,2048]{1,0:T(8,128)(2,1)} copy(bf16[1024,2048]{0,1:T(8,128)(2,1)} %pad_maximum_fusion) | data formatting | bytes 8388608
  503.1 59.8 %psum.15 = f32[6,1024]{1,0:T(8,128)S(1)} all-reduce(f32[6,1024]{1,0:T(8,128)S(1)} %stack.135), channel_id=1, replica_groups=mesh['seq'=16,'head'=2] {'seq'}, use_global_device_ids=true, to_apply=%region_35.36 | all-reduce | flops 6144 | bytes 49152 | tf_op jit(solution)/shard_map/psum | solution.py:583
  584.2 21.6 %reduce-scatter.7.cloned.1.call-done = bf16[64,2048]{1,0:T(8,128)(2,1)} async-done(((bf16[1024,2048]{1,0:T(8,128)(2,1)}), bf16[64,2048]{1,0:T(8,128)(2,1)}) %reduce-scatter.7.cloned.1.call-update) | async-done | bytes 262160
  (382 shorter events, 207.4 us)
Async XLA Ops:
  10.0 21.8 %all-to-all-start = ((bf16[8,128,256]{2,1,0:T(8,128)(2,1)}), bf16[8,128,256]{2,1,0:T(8,128)(2,1)S(1)}, u32[]{:S(2)}, u32[]{:S(2)}) async-start(bf16[8,128,256]{2,1,0:T(8,128)(2,1)} %bitcast.4), calls=%async_computation | async-start | bytes 1048576 | tf_op jit(solution)/shard_map/all_to_all | solution.py:408
  31.8 10.6 %all-to-all-start.1 = ((bf16[4,2,256,128]{3,2,1,0:T(8,128)(2,1)}), bf16[4,2,256,128]{3,2,1,0:T(8,128)(2,1)S(1)}, u32[]{:S(2)}, u32[]{:S(2)}) async-start(bf16[4,2,256,128]{3,2,1,0:T(8,128)(2,1)} %pad_maximum_fusion.6), calls=%async_computation.1 | async-start | bytes 1048576 | tf_op jit(solution)/shard_map/all_to_all | solution.py:413
  35.3 7.2 %collective-permute-start = (bf16[8,128,256]{2,1,0:T(8,128)(2,1)S(1)}, bf16[8,128,256]{2,1,0:T(8,128)(2,1)S(1)}, u32[]{:S(2)}, u32[]{:S(2)}) collective-permute-start(bf16[8,128,256]{2,1,0:T(8,128)(2,1)S(1)} %all-to-all-done.own_q), channel_id=1, source_target_pairs={{0,2},{2,0},{4,6},{6,4},{8,10},{10,8},{12,14},{14,12},{16,18},{18,... | collective-permute-start | bytes 1572872 | tf_op jit(solution)/shard_map/ppermute | solution.py:405
  58.9 2.2 collective-permute-start.1
  84.1 12.5 %collective-permute-start.2 = (bf16[256,1024]{1,0:T(8,128)(2,1)S(1)}, bf16[256,1024]{1,0:T(8,128)(2,1)S(1)}, u32[]{:S(2)}, u32[]{:S(2)}) collective-permute-start(bf16[256,1024]{1,0:T(8,128)(2,1)S(1)} %get-tuple-element.191), channel_id=1, source_target_pairs={{0,1},{1,0},{2,3},{3,2},{4,5},{5,4},{6,7},{7,6},{8,9},{9,8},{10,11... | collective-permute-start | bytes 1572872 | tf_op jit(solution)/shard_map/ppermute | solution.py:418
  99.3 17.8 %all-to-all-start.3 = ((bf16[8,128,256]{2,1,0:T(8,128)(2,1)}), bf16[8,128,256]{2,1,0:T(8,128)(2,1)S(1)}, u32[]{:S(2)}, u32[]{:S(2)}) async-start(bf16[8,128,256]{2,1,0:T(8,128)(2,1)} %bitcast.24), calls=%async_computation.3 | async-start | bytes 1048576 | tf_op jit(solution)/shard_map/all_to_all | solution.py:408
  117.9 21.8 %all-to-all-start.4 = ((bf16[4,2,768,128]{3,2,1,0:T(8,128)(2,1)}), bf16[4,2,768,128]{3,2,1,0:T(8,128)(2,1)S(1)}, u32[]{:S(2)}, u32[]{:S(2)}) async-start(bf16[4,2,768,128]{3,2,1,0:T(8,128)(2,1)} %pad_maximum_fusion.2), calls=%async_computation.4 | async-start | bytes 3145728 | tf_op jit(solution)/shard_map/all_to_all | solution.py:413
  121.7 18.0 %collective-permute-start.3 = (bf16[8,128,256]{2,1,0:T(8,128)(2,1)}, bf16[8,128,256]{2,1,0:T(8,128)(2,1)}, u32[]{:S(2)}, u32[]{:S(2)}) collective-permute-start(bf16[8,128,256]{2,1,0:T(8,128)(2,1)} %copy-done.7), channel_id=1, source_target_pairs={{0,2},{2,0},{4,6},{6,4},{8,10},{10,8},{12,14},{14,12},{16,18},{18,... | collective-permute-start | bytes 1572872 | tf_op jit(solution)/shard_map/ppermute | solution.py:405
  170.6 3.0 collective-permute-start.4
  200.0 12.5 %collective-permute-start.5 = (bf16[256,1024]{1,0:T(8,128)(2,1)S(1)}, bf16[256,1024]{1,0:T(8,128)(2,1)S(1)}, u32[]{:S(2)}, u32[]{:S(2)}) collective-permute-start(bf16[256,1024]{1,0:T(8,128)(2,1)S(1)} %get-tuple-element.193), channel_id=1, source_target_pairs={{0,1},{1,0},{2,3},{3,2},{4,5},{5,4},{6,7},{7,6},{8,9},{9,8},{10,11... | collective-permute-start | bytes 1572872 | tf_op jit(solution)/shard_map/ppermute | solution.py:418
  219.4 11.6 %collective-permute-start.6 = (bf16[256,1024]{1,0:T(8,128)(2,1)S(1)}, bf16[256,1024]{1,0:T(8,128)(2,1)S(1)}, u32[]{:S(2)}, u32[]{:S(2)}) collective-permute-start(bf16[256,1024]{1,0:T(8,128)(2,1)S(1)} %get-tuple-element.195), channel_id=1, source_target_pairs={{0,1},{1,0},{2,3},{3,2},{4,5},{5,4},{6,7},{7,6},{8,9},{9,8},{10,11... | collective-permute-start | bytes 1572872 | tf_op jit(solution)/shard_map/ppermute | solution.py:418
  247.4 10.9 %collective-permute-start.7 = (bf16[256,1024]{1,0:T(8,128)(2,1)}, bf16[256,1024]{1,0:T(8,128)(2,1)}, u32[]{:S(2)}, u32[]{:S(2)}) collective-permute-start(bf16[256,1024]{1,0:T(8,128)(2,1)} %get-tuple-element.197), channel_id=1, source_target_pairs={{0,1},{1,0},{2,3},{3,2},{4,5},{5,4},{6,7},{7,6},{8,9},{9,8},{10,11... | collective-permute-start | bytes 1572872 | tf_op jit(solution)/shard_map/ppermute | solution.py:418
  290.0 2.0 collective-permute-start.8
  325.9 4.0 collective-permute-start.9
  349.6 25.8 %all-to-all-start.11 = ((bf16[4,2,768,128]{3,2,1,0:T(8,128)(2,1)}), bf16[4,2,768,128]{3,2,1,0:T(8,128)(2,1)}, u32[]{:S(2)}, u32[]{:S(2)}) async-start(bf16[4,2,768,128]{3,2,1,0:T(8,128)(2,1)} %get-tuple-element.38), calls=%async_computation.11 | async-start | bytes 3145728 | tf_op jit(solution)/shard_map/all_to_all | solution.py:413
  354.0 141.8 %all-reduce.4.cloned.1.call-start = ((), (), s32[]{:S(2)}) async-start(), calls=%async_computation.14 | async-start | bytes 2097152 | tf_op jit(solution)/shard_map/psum | solution.py:531
  358.4 218.6 %reduce-scatter.9.cloned.1.call-start = ((), (), s32[]{:S(2)}) async-start(), calls=%async_computation.16 | async-start | bytes 4456448
  364.0 31.2 %collective-permute-start.10 = (bf16[256,1024]{1,0:T(8,128)(2,1)}, bf16[256,1024]{1,0:T(8,128)(2,1)S(1)}, u32[]{:S(2)}, u32[]{:S(2)}) collective-permute-start(bf16[256,1024]{1,0:T(8,128)(2,1)} %get-tuple-element.199), channel_id=1, source_target_pairs={{0,1},{1,0},{2,3},{3,2},{4,5},{5,4},{6,7},{7,6},{8,9},{9,8},{10,11... | collective-permute-start | bytes 1572872 | tf_op jit(solution)/shard_map/ppermute | solution.py:418
  444.2 4.5 collective-permute-start.12
  444.2 13.7 %all-to-all-start.10 = ((bf16[4,2,256,128]{3,2,1,0:T(8,128)(2,1)}), bf16[4,2,256,128]{3,2,1,0:T(8,128)(2,1)}, u32[]{:S(2)}, u32[]{:S(2)}) async-start(bf16[4,2,256,128]{3,2,1,0:T(8,128)(2,1)} %copy-done.10), calls=%async_computation.10 | async-start | bytes 1048576 | tf_op jit(solution)/shard_map/all_to_all | solution.py:413
  457.9 18.8 %all-to-all-start.9 = ((bf16[8,128,256]{2,1,0:T(8,128)(2,1)}), bf16[8,128,256]{2,1,0:T(8,128)(2,1)}, u32[]{:S(2)}, u32[]{:S(2)}) async-start(bf16[8,128,256]{2,1,0:T(8,128)(2,1)} %add_convert_fusion), calls=%async_computation.9 | async-start | bytes 1048576 | tf_op jit(solution)/shard_map/all_to_all | solution.py:408
  462.0 143.8 %reduce-scatter.7.cloned.1.call-start = ((), (), s32[]{:S(2)}) async-start(), calls=%async_computation.15 | async-start | bytes 4456448
  494.3 74.1 %collective-permute-start.14 = (bf16[768,1024]{1,0:T(8,128)(2,1)}, bf16[768,1024]{1,0:T(8,128)(2,1)}, u32[]{:S(2)}, u32[]{:S(2)}) collective-permute-start(bf16[768,1024]{1,0:T(8,128)(2,1)} %get-tuple-element.203), channel_id=1, source_target_pairs={{0,1},{1,0},{2,3},{3,2},{4,5},{5,4},{6,7},{7,6},{8,9},{9,8},{10,11... | collective-permute-start | bytes 4718600 | tf_op jit(solution)/shard_map/ppermute | solution.py:418
  566.5 9.4 %collective-permute-start.13 = (bf16[256,1024]{1,0:T(8,128)(2,1)S(1)}, bf16[256,1024]{1,0:T(8,128)(2,1)S(1)}, u32[]{:S(2)}, u32[]{:S(2)}) collective-permute-start(bf16[256,1024]{1,0:T(8,128)(2,1)S(1)} %get-tuple-element.201), channel_id=1, source_target_pairs={{0,1},{1,0},{2,3},{3,2},{4,5},{5,4},{6,7},{7,6},{8,9},{9,8},{10,11... | collective-permute-start | bytes 1572872 | tf_op jit(solution)/shard_map/ppermute | solution.py:418
  (75 other events, 686.3 us)
Sparse Core Ops, SparseCore 0:
  358.5 95.4 all-reduce.3
  457.9 71.9 reduce-scatter.8
  534.2 71.5 reduce-scatter.6

commit v2 on v1

--- a/solution.py
+++ b/solution.py
@@ -34,11 +34,20 @@
     return contract(left, right, 0, 0)
 
 
-def norm_rows(values, norm_gain, norm_bias):
+def norm_parts(values, norm_gain, norm_bias):
     average = jnp.mean(values, axis=-1, keepdims=True)
     centred = values - average
-    spread = jnp.mean(centred * centred, axis=-1, keepdims=True)
-    return centred * lax.rsqrt(spread + 1e-05) * norm_gain + norm_bias
+    scale = lax.rsqrt(jnp.mean(centred * centred, axis=-1, keepdims=True) + 1e-05)
+    unit = centred * scale
+    return unit * norm_gain + norm_bias, (unit, scale, norm_gain)
+
+
+def norm_back(kept, grad):
+    unit, scale, norm_gain = kept
+    scaled = grad * norm_gain
+    first = jnp.mean(scaled, axis=-1, keepdims=True)
+    second = jnp.mean(scaled * unit, axis=-1, keepdims=True)
+    return (scaled - first - unit * second) * scale, jnp.sum(grad * unit, axis=0), jnp.sum(grad, axis=0)
 
 
 class Shape:
@@ -346,6 +355,482 @@
             flops=20 * pairs * HEAD_DIM, bytes_accessed=8 * 1024 * 1024, transcendentals=2 * pairs
         ),
     )(bounds[0], bounds[1], place, own_q, other_q, own_g, other_g, keys_values)
+
+
+class RowShape:
+    def __init__(self, chips, rows, starts):
+        self.chips, self.rows, self.starts = chips, rows, starts
+        self.source_length, self.causal = 2 * chips * rows, True
+        self.span = 2 if chips % 2 == 0 else 1
+        self.tiles = chips // self.span
+        self.tile = self.span * rows
+        self.step = 2 * self.span * rows
+
+
+def own_places(shape, tile, core):
+    lanes = lax.broadcasted_iota(jnp.int32, (1, shape.tile), 1)
+    places = 2 * tile * shape.span * shape.rows + core * shape.rows + lanes
+    for block in range(1, shape.span):
+        places = places + jnp.where(lanes >= block * shape.rows, shape.rows, 0)
+    return places
+
+
+def chip_places(shape, step, core):
+    rows = lax.broadcasted_iota(jnp.int32, (shape.step, shape.tile), 0)
+    places = step * shape.step + rows
+    for block in range(2 * shape.span):
+        here = jnp.logical_and(rows >= block * shape.rows, rows < (block + 1) * shape.rows)
+        shift = shape.rows * core if block % 2 == 0 else -shape.rows * core
+        places = places + jnp.where(here, shift, 0)
+    return places
+
+
+def row_conditions(shape, tile, step, pack, bounds):
+    head = tile * shape.step
+    tail = head + shape.step - 1
+    begin = step * shape.step
+    end = begin + shape.step
+    low_first, _ = position_range(shape, head, pack, bounds, bounds)
+    low_last, _ = position_range(shape, tail, pack, bounds, bounds)
+    some = low_first < end
+    whole = jnp.logical_and(low_last <= begin, end <= head + 1)
+    return some, whole
+
+
+def fill_rows(shape, own_kv, other_kv, which, target, transposed):
+    for chip in range(shape.chips):
+        for side, ref in enumerate((own_kv, other_kv)):
+            first = (2 * chip + side) * shape.rows
+            block = ref[chip, which]
+            if transposed:
+                target[:, first : first + shape.rows] = block.T
+            else:
+                target[first : first + shape.rows, :] = block
+
+
+def tile_lanes(ref, tile, span):
+    return jnp.concatenate([ref[tile * span + block] for block in range(span)], axis=1)
+
+
+def row_forward_kernel(
+    shape, bounds, place, queries, own_kv, other_kv, out, logs, key_all, value_t, maxima, sums, total
+):
+    pack, core = place[0], place[1]
+    fill_rows(shape, own_kv, other_kv, 0, key_all, False)
+    fill_rows(shape, own_kv, other_kv, 1, value_t, True)
+
+    def per_tile(tile, unused):
+        query = tile_lanes(queries, tile, shape.span)
+        low, high = position_range(shape, own_places(shape, tile, core), pack, bounds, bounds)
+        maxima[...] = jnp.full_like(maxima, LOWEST)
+        sums[...] = jnp.zeros_like(sums)
+        total[...] = jnp.zeros_like(total)
+
+        def per_step(step, unused):
+            some, whole = row_conditions(shape, tile, step, pack, bounds)
+            first = pl.multiple_of(step * shape.step, shape.step)
+
+            def fold(masked):
+                key_rows = key_all[pl.ds(first, shape.step), :]
+                if masked:
+                    places = chip_places(shape, step, core)
+                    allowed = jnp.logical_and(places >= low, places < high)
+                for head in range(2):
+                    features = slice(head * HEAD_DIM, (head + 1) * HEAD_DIM)
+                    scores = matrix_product(key_rows, one_head(query, head))
+                    if masked:
+                        scores = jnp.where(allowed, scores, EXCLUDED)
+                    before = maxima[head : head + 1, :]
+                    now = jnp.maximum(before, jnp.max(scores, axis=0, keepdims=True))
+                    weights = jnp.exp(scores - now)
+                    fading = jnp.exp(before - now)
+                    maxima[head : head + 1, :] = now
+                    sums[head : head + 1, :] = sums[head : head + 1, :] * fading + jnp.sum(
+                        weights, axis=0, keepdims=True
+                    )
+                    values = value_t[features, pl.ds(first, shape.step)]
+                    total[features, :] = total[features, :] * fading + matrix_product(
+                        values, weights.astype(BF16)
+                    )
+
+            pl.when(jnp.logical_and(some, whole))(functools.partial(fold, False))
+            pl.when(jnp.logical_and(some, jnp.logical_not(whole)))(functools.partial(fold, True))
+            return 0
+
+        lax.fori_loop(0, tile + 1, per_step, 0)
+        for head in range(2):
+            features = slice(head * HEAD_DIM, (head + 1) * HEAD_DIM)
+            divisor = sums[head : head + 1, :]
+            result = (total[features, :] / divisor).astype(BF16)
+            found = maxima[head : head + 1, :] + jnp.log(divisor)
+            for block in range(shape.span):
+                lanes = slice(block * shape.rows, (block + 1) * shape.rows)
+                out[tile * shape.span + block, features, :] = result[:, lanes]
+                logs[tile * shape.span + block, head : head + 1, :] = found[:, lanes]
+        return 0
+
+    lax.fori_loop(0, shape.tiles, per_tile, 0)
+
+
+def row_backward_kernel(
+    shape, bounds, place, queries, outputs, logs, grads, own_kv, other_kv,
+    query_grads, own_dkv, other_dkv, key_all, value_all, key_t, grad_key, grad_value, grad_query,
+):
+    pack, core = place[0], place[1]
+    fill_rows(shape, own_kv, other_kv, 0, key_all, False)
+    fill_rows(shape, own_kv, other_kv, 1, value_all, False)
+    fill_rows(shape, own_kv, other_kv, 0, key_t, True)
+    grad_key[...] = jnp.zeros_like(grad_key)
+    grad_value[...] = jnp.zeros_like(grad_value)
+
+    def per_tile(tile, unused):
+        query = tile_lanes(queries, tile, shape.span)
+        grad = tile_lanes(grads, tile, shape.span)
+        product = grad.astype(F32) * tile_lanes(outputs, tile, shape.span).astype(F32)
+        log_rows = tile_lanes(logs, tile, shape.span)
+        low, high = position_range(shape, own_places(shape, tile, core), pack, bounds, bounds)
+        heads = []
+        for head in range(2):
+            features = slice(head * HEAD_DIM, (head + 1) * HEAD_DIM)
+            delta = jnp.sum(product[features], axis=0, keepdims=True)
+            heads.append((one_head(query, head), one_head(grad, head), log_rows[head : head + 1], delta))
+        grad_query[...] = jnp.zeros_like(grad_query)
+
+        def per_step(step, unused):
+            some, whole = row_conditions(shape, tile, step, pack, bounds)
+            first = pl.multiple_of(step * shape.step, shape.step)
+
+            def fold(masked):
+                part = pl.ds(first, shape.step)
+                key_rows, value_rows = key_all[part, :], value_all[part, :]
+                if masked:
+                    places = chip_places(shape, step, core)
+                    allowed = jnp.logical_and(places >= low, places < high)
+                probs, diffs = [], []
+                for head in range(2):
+                    head_query, head_grad, log_row, delta = heads[head]
+                    features = slice(head * HEAD_DIM, (head + 1) * HEAD_DIM)
+                    scores = matrix_product(key_rows, head_query)
+                    if masked:
+                        scores = jnp.where(allowed, scores, EXCLUDED)
+                    weights = jnp.exp(scores - log_row)
+                    change = matrix_product(value_rows, head_grad)
+                    diff = (weights * (change - delta)).astype(BF16)
+                    grad_query[features, :] += matrix_product(key_t[features, part], diff)
+                    probs.append(weights.astype(BF16))
+                    diffs.append(diff)
+                grad_key[part, :] += times_transposed(
+                    jnp.concatenate(diffs, axis=1),
+                    jnp.concatenate([heads[0][0], heads[1][0]], axis=1),
+                )
+                grad_value[part, :] += times_transposed(
+                    jnp.concatenate(probs, axis=1),
+                    jnp.concatenate([heads[0][1], heads[1][1]], axis=1),
+                )
+
+            pl.when(jnp.logical_and(some, whole))(functools.partial(fold, False))
+            pl.when(jnp.logical_and(some, jnp.logical_not(whole)))(functools.partial(fold, True))
+            return 0
+
+        lax.fori_loop(0, tile + 1, per_step, 0)
+        result = (grad_query[...] * HEAD_DIM**-0.5).astype(BF16)
+        for block in range(shape.span):
+            query_grads[tile * shape.span + block] = result[
+                :, block * shape.rows : (block + 1) * shape.rows
+            ]
+        return 0
+
+    lax.fori_loop(0, shape.tiles, per_tile, 0)
+    for chip in range(shape.chips):
+        for side, ref in enumerate((own_dkv, other_dkv)):
+            first = (2 * chip + side) * shape.rows
+            ref[chip, 0] = grad_key[first : first + shape.rows, :].astype(BF16)
+            ref[chip, 1] = grad_value[first : first + shape.rows, :].astype(BF16)
+
+
+def row_forward(shape, bounds, place, queries, own_kv, other_kv):
+    length = shape.source_length
+    return pl.pallas_call(
+        functools.partial(row_forward_kernel, shape),
+        out_shape=(
+            jax.ShapeDtypeStruct(queries.shape, BF16),
+            jax.ShapeDtypeStruct((shape.chips, 2, shape.rows), F32),
+        ),
+        in_specs=[smem()] * 2 + [vmem()] * 3,
+        out_specs=(vmem(), vmem()),
+        scratch_shapes=[
+            pltpu.VMEM((length, PAIR), BF16),
+            pltpu.VMEM((PAIR, length), BF16),
+            pltpu.VMEM((8, shape.tile), F32),
+            pltpu.VMEM((8, shape.tile), F32),
+            pltpu.VMEM((PAIR, shape.tile), F32),
+        ],
+        compiler_params=pltpu.CompilerParams(**PARAMS),
+        cost_estimate=pl.CostEstimate(
+            flops=6 * length * length * HEAD_DIM,
+            bytes_accessed=4 * 1024 * 1024,
+            transcendentals=length * length,
+        ),
+    )(bounds, place, queries, own_kv, other_kv)
+
+
+def row_backward(shape, bounds, place, queries, outputs, logs, grads, own_kv, other_kv):
+    length = shape.source_length
+    return pl.pallas_call(
+        functools.partial(row_backward_kernel, shape),
+        out_shape=(
+            jax.ShapeDtypeStruct(queries.shape, BF16),
+            jax.ShapeDtypeStruct(own_kv.shape, BF16),
+            jax.ShapeDtypeStruct(own_kv.shape, BF16),
+        ),
+        in_specs=[smem()] * 2 + [vmem()] * 6,
+        out_specs=(vmem(), vmem(), vmem()),
+        scratch_shapes=[
+            pltpu.VMEM((length, PAIR), BF16),
+            pltpu.VMEM((length, PAIR), BF16),
+            pltpu.VMEM((PAIR, length), BF16),
+            pltpu.VMEM((length, PAIR), F32),
+            pltpu.VMEM((length, PAIR), F32),
+            pltpu.VMEM((PAIR, shape.tile), F32),
+        ],
+        compiler_params=pltpu.CompilerParams(**PARAMS),
+        cost_estimate=pl.CostEstimate(
+            flops=12 * length * length * HEAD_DIM,
+            bytes_accessed=6 * 1024 * 1024,
+            transcendentals=length * length,
+        ),
+    )(bounds, place, queries, outputs, logs, grads, own_kv, other_kv)
+
+
+def blocks(array):
+    return pl.BlockSpec(array.shape, lambda step, zeros=(0,) * array.ndim: zeros)
+
+
+def call(kernel, out_shape, args, grid=None, in_specs=None, out_specs=None, scratch=(), flops=0):
+    if in_specs is None:
+        in_specs = [vmem()] * len(args)
+    if out_specs is None:
+        out_specs = jax.tree.map(lambda _: vmem(), out_shape)
+    extra = {} if grid is None else {"grid": grid}
+    return pl.pallas_call(
+        kernel,
+        out_shape=out_shape,
+        in_specs=in_specs,
+        out_specs=out_specs,
+        scratch_shapes=list(scratch),
+        compiler_params=pltpu.CompilerParams(**PARAMS),
+        cost_estimate=pl.CostEstimate(flops=flops, bytes_accessed=8 << 20, transcendentals=0),
+        **extra,
+    )(*args)
+
+
+def project_self(x, wq, wk, wv, packs):
+    rows, width = x.shape[0], wq.shape[1]
+    pairs, each = width // PAIR, rows // packs
+
+    def kernel(x_ref, wq_ref, wk_ref, wv_ref, out):
+        value = x_ref[...]
+        query = (matrix_product(value, wq_ref[...]) * HEAD_DIM**-0.5).astype(BF16)
+        for pack in range(packs):
+            for pair in range(pairs):
+                part = query[pack * each : (pack + 1) * each, pair * PAIR : (pair + 1) * PAIR]
+                out[pack * pairs + pair, 0] = part.T
+        for number, ref in ((1, wk_ref), (2, wv_ref)):
+            result = matrix_product(value, ref[...]).astype(BF16)
+            for pack in range(packs):
+                for pair in range(pairs):
+                    out[pack * pairs + pair, number] = result[
+                        pack * each : (pack + 1) * each, pair * PAIR : (pair + 1) * PAIR
+                    ]
+
+    return call(
+        kernel,
+        jax.ShapeDtypeStruct((packs * pairs, 3, each, PAIR), BF16),
+        (x, wq, wk, wv),
+        flops=6 * rows * x.shape[1] * width,
+    )
+
+
+def project_sources(x, wk, wv):
+    rows, depth = x.shape
+    pairs = wk.shape[1] // PAIR
+    size = rows // 3 if rows % 48 == 0 else rows
+
+    def kernel(x_ref, wk_ref, wv_ref, out):
+        for number, ref in enumerate((wk_ref, wv_ref)):
+            result = matrix_product(x_ref[...], ref[...]).astype(BF16)
+            for pair in range(pairs):
+                out[pair, number] = result[:, pair * PAIR : (pair + 1) * PAIR]
+
+    return call(
+        kernel,
+        jax.ShapeDtypeStruct((pairs, 2, rows, PAIR), BF16),
+        (x, wk, wv),
+        grid=(rows // size,),
+        in_specs=[pl.BlockSpec((size, depth), lambda i: (i, 0)), blocks(wk), blocks(wv)],
+        out_specs=pl.BlockSpec((pairs, 2, size, PAIR), lambda i: (0, 0, i, 0)),
+        flops=4 * rows * depth * wk.shape[1],
+    )
+
+
+def source_grads(grads, wk, wv):
+    pairs, _, rows, _ = grads.shape
+    size = rows // 3 if rows % 48 == 0 else rows
+    depth = wk.shape[0]
+
+    def kernel(grads_ref, wk_ref, wv_ref, out):
+        keys = jnp.concatenate([grads_ref[pair, 0] for pair in range(pairs)], axis=1)
+        values = jnp.concatenate([grads_ref[pair, 1] for pair in range(pairs)], axis=1)
+        total = times_transposed(keys, wk_ref[...]) + times_transposed(values, wv_ref[...])
+        out[...] = total.astype(BF16)
+
+    return call(
+        kernel,
+        jax.ShapeDtypeStruct((rows, depth), BF16),
+        (grads, wk, wv),
+        grid=(rows // size,),
+        in_specs=[
+            pl.BlockSpec((pairs, 2, size, PAIR), lambda i: (0, 0, i, 0)),
+            blocks(wk),
+            blocks(wv),
+        ],
+        out_specs=pl.BlockSpec((size, depth), lambda i: (i, 0)),
+        flops=4 * rows * depth * wk.shape[1],
+    )
+
+
+def input_grads(back, wq, wk, wv, packs):
+    pairs = back.shape[0] // packs
+    each = back.shape[3]
+    depth = wq.shape[0]
+
+    def kernel(back_ref, wq_ref, wk_ref, wv_ref, out):
+        for pack in range(packs):
+            first = pack * pairs
+            parts = [
+                jnp.concatenate([back_ref[first + pair, 0].T for pair in range(pairs)], axis=1),
+                jnp.concatenate([back_ref[first + pair, 1] for pair in range(pairs)], axis=1),
+                jnp.concatenate([back_ref[first + pair, 2] for pair in range(pairs)], axis=1),
+            ]
+            total = times_transposed(parts[0], wq_ref[...])
+            total += times_transposed(parts[1], wk_ref[...])
+            total += times_transposed(parts[2], wv_ref[...])
+            out[pack * each : (pack + 1) * each, :] = total.astype(BF16)
+
+    return call(
+        kernel,
+        jax.ShapeDtypeStruct((packs * each, depth), BF16),
+        (back, wq, wk, wv),
+        flops=6 * packs * each * depth * wq.shape[1],
+    )
+
+
+def self_weight_grads(x, back, packs):
+    pairs = back.shape[0] // packs
+    rows, depth = x.shape
+    width = pairs * PAIR
+
+    def kernel(x_ref, back_ref, out):
+        value = x_ref[...].T
+        each = rows // packs
+        for number in range(3):
+            for pair in range(pairs):
+                column = number * width + pair * PAIR
+                if number == 0:
+                    other = jnp.concatenate(
+                        [back_ref[pack * pairs + pair, 0] for pack in range(packs)], axis=1
+                    )
+                    result = times_transposed(value, other)
+                else:
+                    other = jnp.concatenate(
+                        [back_ref[pack * pairs + pair, number] for pack in range(packs)], axis=0
+                    )
+                    result = matrix_product(value, other)
+                out[:, column : column + PAIR] = result.astype(BF16)
+
+    return call(
+        kernel,
+        jax.ShapeDtypeStruct((depth, 3 * width), BF16),
+        (x, back),
+        flops=2 * rows * depth * 3 * width,
+    )
+
+
+def middle_weight_grads(
+    second, mixed_cross, first, mixed_self, one, query_grads, source, source_dkv,
+    third, narrow, two, narrow_grads,
+):
+    depth = second.shape[1]
+    width = mixed_cross.shape[0]
+    pairs = width // PAIR
+
+    def kernel(
+        second_ref, cross_ref, first_ref, self_ref, one_ref, query_ref, source_ref, dkv_ref,
+        third_ref, narrow_ref, two_ref, dnarrow_ref, out,
+    ):
+        step = pl.program_id(0)
+
+        def rows_by_features(left, right):
+            out[...] = times_transposed(left[...].T, right[...]).astype(BF16)
+
+        pl.when(step == 0)(lambda: rows_by_features(second_ref, cross_ref))
+        pl.when(step == 1)(lambda: rows_by_features(first_ref, self_ref))
+        pl.when(step == 2)(lambda: rows_by_features(one_ref, query_ref))
+
+        def sources(number):
+            right = jnp.concatenate([dkv_ref[pair, number] for pair in range(pairs)], axis=1)
+            out[...] = matrix_product(source_ref[...].T, right).astype(BF16)
+
+        pl.when(step == 3)(lambda: sources(0))
+        pl.when(step == 4)(lambda: sources(1))
+
+        def adapters():
+            half = narrow_ref.shape[1]
+            up = 4.0 * matrix_product(third_ref[...].T, narrow_ref[...])
+            out[:, :half] = up.astype(BF16)
+            out[:, half:] = matrix_product(two_ref[...].T, dnarrow_ref[...]).astype(BF16)
+
+        pl.when(step == 5)(adapters)
+
+    args = (
+        second, mixed_cross, first, mixed_self, one, query_grads, source, source_dkv,
+        third, narrow, two, narrow_grads,
+    )
+    return call(
+        kernel,
+        jax.ShapeDtypeStruct((depth, 6 * width), BF16),
+        args,
+        grid=(6,),
+        in_specs=[blocks(value) for value in args],
+        out_specs=pl.BlockSpec((depth, width), lambda i: (0, i)),
+        flops=2 * depth * width * 2560,
+    )
+
+
+def cross_message(second, weight, attended, logs):
+    rows = second.shape[0]
+    pairs = weight.shape[0] // PAIR
+
+    def kernel(second_ref, weight_ref, attended_ref, logs_ref, out):
+        for pair in range(pairs):
+            grads = times_transposed(weight_ref[pair * PAIR : (pair + 1) * PAIR, :], second_ref[...])
+            low = grads.astype(BF16)
+            out[pair, :PAIR, :] = low
+            low = low.astype(F32)
+            first, later = [], []
+            for side in range(2):
+                head = 2 * pair + side
+                product = low[side * HEAD_DIM : (side + 1) * HEAD_DIM] * attended_ref[head]
+                first.extend(split_low(logs_ref[head : head + 1, :]))
+                later.extend(split_low(jnp.sum(product, axis=0, keepdims=True)))
+            out[pair, PAIR : PAIR + STATS, :] = stat_rows(first + later, rows)
+
+    return call(
+        kernel,
+        jax.ShapeDtypeStruct((pairs, PAIR + STATS, rows), BF16),
+        (second, weight, attended, logs),
+        flops=2 * rows * weight.shape[0] * weight.shape[1],
+    )
 
 
 def on_device(
@@ -387,6 +872,9 @@
     core = position % 2
     base = position // (2 * pairs_here) * (2 * pairs_here)
     place = jnp.stack([base, core]).astype(jnp.int32)
+    by_pack = pairs_here * pack_count == chips and head_size == 2
+    row_place = jnp.stack([position // (2 * pairs_here), core]).astype(jnp.int32)
+    row_shape = RowShape(chips, row_count, starts)
     self_bounds = (tgt_bounds.reshape(-1), tgt_bounds.reshape(-1))
     cross_bounds = (tgt_bounds.reshape(-1), src_bounds.reshape(-1))
     self_shape = Shape(chips, pairs_here, pack_count, row_count, row_count, starts, True)
@@ -417,6 +905,12 @@
             low = lax.reduce_precision(value, 8, 7)
             return low + lax.ppermute(low.astype(BF16), "head", [(0, 1), (1, 0)]).astype(F32)
         return lax.psum(value, "head")
+
+    def head_sum_low(low):
+        if head_size == 2:
+            met = lax.ppermute(low, "head", [(0, 1), (1, 0)])
+            return low.astype(F32) + met.astype(F32)
+        return lax.psum(low.astype(F32), "head")
 
     def spread_queries(features):
         message = features.reshape(pairs_here, -1, rows)
@@ -482,29 +976,37 @@
         return jnp.sum(back.astype(F32), axis=0).astype(BF16)
 
     scaling = HEAD_DIM**-0.5
-    query_self = (contract(self_query, flat_inputs, 0, 1) * scaling).astype(BF16)
-    key_self = matrix_product(flat_inputs, self_key).astype(BF16)
-    value_self = matrix_product(flat_inputs, self_value).astype(BF16)
-    self_q = spread_queries(query_self)
-    self_kv = to_near(pair_rows(key_self, value_self))
-    own_part, other_part = attention_forward(self_shape, self_bounds, place, *self_q, self_kv)
-    attended_self, log_self = collect(own_part, other_part)
-    mixed_self = attended_self.reshape(local_width, rows).astype(BF16)
+    cross_kv = to_near(project_sources(flat_encoded, cross_key, cross_value))
+    if by_pack:
+        message = project_self(flat_inputs, self_query, self_key, self_value, pack_count)
+        met = to_all(message)
+        self_q, self_kv = met[:, 0], met[:, 1:]
+        self_kv_other = swap_core(self_kv)
+        self_heads, self_logs = row_forward(
+            row_shape, self_bounds[0], row_place, self_q, self_kv, self_kv_other
+        )
+        self_heads, cross_kv = lax.optimization_barrier((self_heads, cross_kv))
+        back = to_all(self_heads).reshape(pack_count, pairs_here, PAIR, row_count)
+        mixed_self = back.transpose(1, 2, 0, 3).reshape(local_width, rows)
+    else:
+        query_self = (contract(self_query, flat_inputs, 0, 1) * scaling).astype(BF16)
+        key_self = matrix_product(flat_inputs, self_key).astype(BF16)
+        value_self = matrix_product(flat_inputs, self_value).astype(BF16)
+        self_q = spread_queries(query_self)
+        self_kv = to_near(pair_rows(key_self, value_self))
+        own_part, other_part = attention_forward(self_shape, self_bounds, place, *self_q, self_kv)
+        attended_self, log_self = collect(own_part, other_part)
+        mixed_self = attended_self.reshape(local_width, rows).astype(BF16)
     out_self = head_sum(transposed_times(mixed_self, self_out))
-    normed_one, norm_one_back = jax.vjp(
-        norm_rows, flat_inputs.astype(F32) + out_self, norm1_gain, norm1_bias
-    )
+    normed_one, norm_one_back = norm_parts(flat_inputs.astype(F32) + out_self, norm1_gain, norm1_bias)
     normed_one_low = normed_one.astype(BF16)
     query_cross = (contract(cross_query, normed_one_low, 0, 1) * scaling).astype(BF16)
-    key_cross = matrix_product(flat_encoded, cross_key).astype(BF16)
-    value_cross = matrix_product(flat_encoded, cross_value).astype(BF16)
-    cross_kv = to_near(pair_rows(key_cross, value_cross))
     cross_q = spread_queries(query_cross)
     own_part, other_part = attention_forward(cross_shape, cross_bounds, place, *cross_q, cross_kv)
     attended_cross, log_cross = collect(own_part, other_part)
     mixed_cross = attended_cross.reshape(local_width, rows).astype(BF16)
     out_cross = head_sum(transposed_times(mixed_cross, cross_out))
-    normed_two, norm_two_back = jax.vjp(norm_rows, normed_one + out_cross, norm2_gain, norm2_bias)
+    normed_two, norm_two_back = norm_parts(normed_one + out_cross, norm2_gain, norm2_bias)
     normed_two_low = normed_two.astype(BF16)
     hidden = matrix_product(normed_two_low, ffn_in)
     activated, gelu_hidden_back = jax.vjp(jax.nn.gelu, hidden)
@@ -516,71 +1018,126 @@
         narrow_low, adapter_up
     )
     branch = head_sum(branch_part)
-    normed_three, norm_three_back = jax.vjp(norm_rows, normed_two + branch, norm3_gain, norm3_bias)
-    grad_third, grad_gain_three, grad_bias_three = norm_three_back(
-        cotangent.reshape(rows, model_width).astype(F32)
+    normed_three, norm_three_back = norm_parts(normed_two + branch, norm3_gain, norm3_bias)
+    grad_third, grad_gain_three, grad_bias_three = norm_back(
+        norm_three_back, cotangent.reshape(rows, model_width).astype(F32)
     )
     grad_branch = grad_third.astype(BF16)
     grad_hidden = gelu_hidden_back(times_transposed(grad_branch, ffn_out))[0].astype(BF16)
     grad_narrow = gelu_narrow_back(4.0 * times_transposed(grad_branch, adapter_up))[0].astype(BF16)
-    grad_adapter_up = 4.0 * transposed_times(narrow_low, grad_branch)
-    grad_adapter_down_t = transposed_times(grad_narrow, normed_two_low)
     grad_two_part = times_transposed(grad_hidden, ffn_in) + times_transposed(
         grad_narrow, adapter_down
     )
-    adapters = lax.psum(
-        jnp.concatenate([grad_adapter_up, grad_adapter_down_t], axis=0).astype(BF16), "seq"
-    ).astype(F32)
     grad_two = grad_third + head_sum(grad_two_part)
-    grad_second, grad_gain_two, grad_bias_two = norm_two_back(grad_two)
+    grad_second, grad_gain_two, grad_bias_two = norm_back(norm_two_back, grad_two)
     grad_second_low = grad_second.astype(BF16)
-    grad_cross_out_t = contract(grad_second_low, mixed_cross, 0, 1)
-    grad_mixed_cross = times_transposed(cross_out, grad_second_low).astype(BF16)
-    cross_g = spread_grads(grad_mixed_cross, attended_cross, log_cross)
+    message = cross_message(
+        grad_second_low, cross_out, attended_cross.reshape(-1, HEAD_DIM, rows), log_cross.reshape(-1, rows)
+    )
+    cross_g = spread_queries(message)
     own_part, other_part, cross_dkv = attention_backward(
         cross_shape, cross_bounds, place, *cross_q, *cross_g, cross_kv
     )
     grad_query_cross = collect_query_grads(own_part, other_part)
-    grad_key_cross, grad_value_cross = join_rows(to_near(cross_dkv))
+    source_dkv = to_near(cross_dkv)
     grad_one_sum = head_sum(transposed_times(grad_query_cross, contract_t(cross_query)))
-    grad_source = head_sum(
-        times_transposed(grad_key_cross, cross_key) + times_transposed(grad_value_cross, cross_value)
-    )
-    grad_cross_query = contract(normed_one_low, grad_query_cross, 0, 1)
-    grad_cross_key = transposed_times(flat_encoded, grad_key_cross)
-    grad_cross_value = transposed_times(flat_encoded, grad_value_cross)
-    grad_first, grad_gain_one, grad_bias_one = norm_one_back(grad_second + grad_one_sum)
+    grad_first, grad_gain_one, grad_bias_one = norm_back(norm_one_back, grad_second + grad_one_sum)
     grad_first_low = grad_first.astype(BF16)
-    grad_self_out_t = contract(grad_first_low, mixed_self, 0, 1)
     grad_mixed_self = times_transposed(self_out, grad_first_low).astype(BF16)
-    self_g = spread_grads(grad_mixed_self, attended_self, log_self)
-    own_part, other_part, self_dkv = attention_backward(
-        self_shape, self_bounds, place, *self_q, *self_g, self_kv
-    )
-    grad_query_self = collect_query_grads(own_part, other_part)
-    grad_key_self, grad_value_self = join_rows(to_near(self_dkv))
-    grad_in_part = (
-        transposed_times(grad_query_self, contract_t(self_query))
-        + times_transposed(grad_key_self, self_key)
-        + times_transposed(grad_value_self, self_value)
-    )
-    grad_inputs = grad_first + head_sum(grad_in_part)
-    grad_self_query = contract(flat_inputs, grad_query_self, 0, 1)
-    grad_self_key = transposed_times(flat_inputs, grad_key_self)
-    grad_self_value = transposed_times(flat_inputs, grad_value_self)
-
-    def scatter(parts):
-        joined = jnp.concatenate([part.astype(BF16) for part in parts], axis=1)
-        scattered = lax.psum_scatter(joined, "seq", scatter_dimension=0, tiled=True).astype(F32)
-        return jnp.split(scattered, len(parts), axis=1)
-
-    cross_out_t, cross_query_g, cross_key_g, cross_value_g = scatter(
-        [grad_cross_out_t, grad_cross_query, grad_cross_key, grad_cross_value]
-    )
-    self_out_t, self_query_g, self_key_g, self_value_g = scatter(
-        [grad_self_out_t, grad_self_query, grad_self_key, grad_self_value]
-    )
-    small = lax.psum(
+    grad_source = head_sum_low(source_grads(source_dkv, cross_key, cross_value))
+    middle = middle_weight_grads(
+        grad_second_low, mixed_cross, grad_first_low, mixed_self, normed_one_low, grad_query_cross,
+        flat_encoded, source_dkv, grad_branch, narrow_low, normed_two_low, grad_narrow,
+    )
+    if by_pack:
+        message = grad_mixed_self.reshape(pairs_here, PAIR, pack_count, row_count)
+        grad_heads = to_all(message.transpose(2, 0, 1, 3).reshape(chips, PAIR, row_count))
+        grad_heads, middle = lax.optimization_barrier((grad_heads, middle))
+        dq, own_dkv, other_dkv = row_backward(
+            row_shape, self_bounds[0], row_place, self_q, self_heads, self_logs, grad_heads,
+            self_kv, self_kv_other,
+        )
+        dkv = (own_dkv.astype(F32) + swap_core(other_dkv).astype(F32)).astype(BF16)
+        back = to_all(jnp.concatenate([dq[:, None], dkv], axis=1))
+        grad_inputs = grad_first + head_sum_low(
+            input_grads(back, self_query, self_key, self_value, pack_count)
+        )
+        self_parts = self_weight_grads(flat_inputs, back, pack_count)
+    else:
+        self_g = spread_grads(grad_mixed_self, attended_self, log_self)
+        own_part, other_part, self_dkv = attention_backward(
+            self_shape, self_bounds, place, *self_q, *self_g, self_kv
+        )
+        grad_query_self = collect_query_grads(own_part, other_part)
+        grad_key_self, grad_value_self = join_rows(to_near(self_dkv))
+        grad_in_part = (
+            transposed_times(grad_query_self, contract_t(self_query))
+            + times_transposed(grad_key_self, self_key)
+            + times_transposed(grad_value_self, self_value)
+        )
+        grad_inputs = grad_first + head_sum(grad_in_part)
+        grad_self_query = contract(flat_inputs, grad_query_self, 0, 1)
+        grad_self_key = transposed_times(flat_inputs, grad_key_self)
+        grad_self_value = transposed_times(flat_inputs, grad_value_self)
+        self_parts = jnp.concatenate(
+            [part.astype(BF16) for part in (grad_self_query, grad_self_key, grad_self_value)], axis=1
+        )
+
+    def scatter(joined):
+        return lax.psum_scatter(joined, "seq", scatter_dimension=0, tiled=True)
+
+    def step(values, bit, axis):
+        mine = position // bit % 2
+
+        def half(which):
+            return [lax.dynamic_index_in_dim(value, which, axis, keepdims=False) for value in values]
+
+        send = sum(value.astype(F32) for value in half(1 - mine)).astype(BF16)
+        met = lax.ppermute(send, "seq", [(i, i ^ bit) for i in range(seq_size)])
+        return half(mine) + [met]
+
+    def scatter_by_halves(joined):
+        if seq_size != 16:
+            return scatter(joined)
+        width = joined.shape[1]
+        values = step([joined.reshape(2, 2, 2, 2, -1, width)], 1, 3)
+        first = [value[..., : width // 2] for value in values]
+        second = [value[..., width // 2 :] for value in values]
+        first, second = step(first, 2, 2), step(second, 4, 1)
+        first, second = step(first, 4, 1), step(second, 2, 1)
+        first, second = step(first, 8, 0), step(second, 8, 0)
+        return jnp.concatenate(
+            [sum(value.astype(F32) for value in part) for part in (first, second)], axis=-1
+        )
+
+    def gather_by_doubling(piece):
+        if seq_size != 16:
+            return lax.all_gather(piece, "seq", axis=0, tiled=True)
+        value = piece
+        for number, bit in enumerate((8, 4, 2, 1)):
+            met = lax.ppermute(value, "seq", [(i, i ^ bit) for i in range(seq_size)])
+            low = position // bit % 2 == 0
+            value = jnp.stack(
+                [jnp.where(low, value, met), jnp.where(low, met, value)], axis=number
+            )
+        return value.reshape(-1, piece.shape[1])
+
+    def sum_small(value):
+        bit = 1
+        while bit < seq_size:
+            value = value + lax.ppermute(value, "seq", [(i, i ^ bit) for i in range(seq_size)])
+            bit *= 2
+        return value
+
+    middle = scatter(middle)
+    adapters = gather_by_doubling(middle[:, 5 * local_width :]).astype(F32)
+    cross_out_t, self_out_t, cross_query_g, cross_key_g, cross_value_g = jnp.split(
+        middle[:, : 5 * local_width].astype(F32), 5, axis=1
+    )
+    self_query_g, self_key_g, self_value_g = jnp.split(
+        scatter_by_halves(self_parts).astype(F32), 3, axis=1
+    )
+    small = sum_small(
         jnp.stack(
             [
                 grad_gain_one,
@@ -590,8 +1147,7 @@
                 grad_gain_three,
                 grad_bias_three,
             ]
-        ),
-        "seq",
+        )
     )
     half = adapter_up.shape[0]
     return (
@@ -606,8 +1162,8 @@
         cross_key_g,
         cross_value_g,
         cross_out_t.T,
-        adapters[half:].T,
-        adapters[:half],
+        adapters[:, half:],
+        adapters[:, :half].T,
         small[0],
         small[1],
         small[2],

time: 628 us -> 514 us (0.82)
  blocking collectives: 162 us -> 90.2 us
  matrix products: 55.4 us -> 19.8 us
  local copies, waits for them, and re-layouts: 74 us -> 45.5 us
  waiting for transfers between devices: 133 us -> 155 us
  other arithmetic: 39.6 us -> 27.5 us
  Pallas kernels: 94.3 us -> 105 us
    psum x1 -> x0, blocking collectives: 59.8 us -> none  [on_device(): lax.psum(jnp.stack([grad_gain_one, grad_bias_one, grad_gain_two, grad_bia...]
    ppermute x0 -> x17, waiting for transfers between devices: none -> 44.8 us  [the longest x2 16.7 us: head_sum_low(): met = lax.ppermute(low, 'head', [(0, 1), (1, 0)])]
    pallas_call x0 -> x9, Pallas kernels: none -> 42.6 us  [the longest x7 19.3 us: call(): pl.pallas_call(kernel, out_shape=out_shape, in_specs=in_specs, out_specs=...]
    all_to_all x4 -> x2, waiting for transfers between devices: 40.2 us -> 3.54 us  [to_near(): lax.all_to_all(value, 'seq', 0, 0, axis_index_groups=near_chips, tiled=True)]
    all_to_all x3, waiting for transfers between devices: 17.4 us -> 46 us  [to_all(): lax.all_to_all(value, 'seq', 0, 0, axis_index_groups=all_chips, tiled=True)]
    dot_general x25 -> x8, matrix products: 43.6 us -> 15.8 us  [contract(): lax.dot_general(left, right, (((left_dim,), (right_dim,)), ((), ())), pre...]
    unnamed x5 -> x1, waiting for transfers between devices: 21.7 us -> 0.02 us
    pallas_call x2 -> x1, Pallas kernels: 50.3 us -> 32.8 us  [attention_backward(): pl.pallas_call(functools.partial(backward_kernel, shape), out_shape=(mess...]
  transfers between devices with their start and end apart: 25 -> 34, of which waited for: 18 -> 24; matrix products, arithmetic and copies ran while one was open for 17% -> 6% of each run, Pallas kernels for 3% -> 8%
where the time goes in v2:
time: 514 us; the launch traced here: 504 us
  waiting for transfers between devices  155 us (30%)
  Pallas kernels  105 us (20%)
  blocking collectives  90.2 us (18%)
  local copies, waits for them, and re-layouts  45.5 us (9%)
  starting transfers between devices  45.5 us (9%)
  other arithmetic  27.5 us (5%)
  matrix products  19.8 us (4%)
  between operations  15.6 us (3%)
    all_to_all x5, blocking collectives, to_all(): lax.all_to_all(value, 'seq', 0, 0, axis_index_groups=all_chips, tiled=True)  90.2 us
    ppermute x5, waiting for transfers between devices, head_sum(): lax.ppermute(low.astype(BF16), 'head', [(0, 1), (1, 0)]).astype(F32)  51.1 us
    all_to_all x3, waiting for transfers between devices, to_all(): lax.all_to_all(value, 'seq', 0, 0, axis_index_groups=all_chips, tiled=True)  46 us
    pallas_call x1, Pallas kernels, attention_backward(): pl.pallas_call(functools.partial(backward_kernel, shape), out_shape=(mess...  32.8 us
    unnamed x175, local copies, waits for them, and re-layouts  30.9 us
    pallas_call x1, Pallas kernels, attention_forward(): pl.pallas_call(functools.partial(forward_kernel, shape), out_shape=(messa...  29.5 us
    pallas_call x7, Pallas kernels, call(): pl.pallas_call(kernel, out_shape=out_shape, in_specs=in_specs, out_specs=...  19.3 us
    ppermute x2, waiting for transfers between devices, head_sum_low(): met = lax.ppermute(low, 'head', [(0, 1), (1, 0)])  16.7 us
  transfers between devices with their start and end apart: 34, of which 24 were waited for; matrix products, arithmetic and copies ran while one was open for 6% of the time, Pallas kernels for 8%

profile of v2, /device:TPU:0, one launch (start us, length us, event | category | flops | bytes accessed | tf_op | source)
XLA Modules:
  0.0 503.8 jit_solution(6641999780414199690)
XLA Ops:
  13.9 7.3 %all-to-all-start = ((bf16[8,3,128,128]{3,2,1,0:T(8,128)(2,1)}), bf16[8,3,128,128]{3,2,1,0:T(8,128)(2,1)S(1)}, u32[]{:S(2)}, u32[]{:S(2)}) async-start(bf16[8,3,128,128]{3,2,1,0:T(8,128)(2,1)} %shard_map.366), calls=%async_computation | async-start | bytes 1572864 | tf_op jit(solution)/shard_map/all_to_all | solution.py:896
  27.0 14.3 %all-to-all-done = bf16[8,3,128,128]{3,2,1,0:T(8,128)(2,1)S(1)} async-done(((bf16[8,3,128,128]{3,2,1,0:T(8,128)(2,1)}), bf16[8,3,128,128]{3,2,1,0:T(8,128)(2,1)S(1)}, u32[]{:S(2)}, u32[]{:S(2)}) %all-to-all-start) | async-done | bytes 786464 | tf_op jit(solution)/shard_map/all_to_all | solution.py:896
  49.0 10.9 %shard_map.367 = (bf16[8,128,128]{2,1,0:T(8,128)(2,1)S(1)}, f32[8,2,128]{2,1,0:T(2,128)S(1)}) custom-call(s32[6]{0:T(128)S(1)} %reshape.329.bounds.target_bounds, s32[2]{0:T(128)S(1)} %pad_add_fusion.place, bf16[8,128,128]{2,1,0:T(8,128)(2,1)S(1)} %slice_bitcast_fusion.1.queries, bf16[8,2,128,128]{3,2,1,0:T(8,128)(2,1)S(1)} %slice.109.own_kv, ...), custom_call_target="tpu_custom_call" | custom-call | flops 1610612736 | bytes 4194304 | tf_op jit(solution)/shard_map/pallas_call | solution.py:553
  64.1 12.7 %all_to_all.50 = bf16[8,128,128]{2,1,0:T(8,128)(2,1)S(1)} all-to-all(bf16[8,128,128]{2,1,0:T(8,128)(2,1)S(1)} %get-tuple-element.34.outputs), channel_id=1, replica_groups={{0,4,8,12,16,20,24,28},{2,6,10,14,18,22,26,30},{1,5,9,13,17,21,25,29},{..., dimensions={0} | all-to-all | bytes 524288 | tf_op jit(solution)/shard_map/all_to_all | solution.py:896
  80.4 10.5 %collective-permute-done.1 = bf16[256,1024]{1,0:T(8,128)(2,1)S(1)} collective-permute-done((bf16[256,1024]{1,0:T(8,128)(2,1)S(1)}, bf16[256,1024]{1,0:T(8,128)(2,1)S(1)}, u32[]{:S(2)}, u32[]{:S(2)}) %collective-permute-start.1) | collective-permute-done | bytes 524320 | tf_op jit(solution)/shard_map/ppermute | solution.py:906
  93.9 18.4 %all_to_all.51.own_q = bf16[8,128,256]{2,1,0:T(8,128)(2,1)S(1)} all-to-all(bf16[8,128,256]{2,1,0:T(8,128)(2,1)S(1)} %bitcast.226), channel_id=1, replica_groups={{0,4,8,12,16,20,24,28},{2,6,10,14,18,22,26,30},{1,5,9,13,17,21,25,29},{..., dimensions={0} | all-to-all | bytes 1048576 | tf_op jit(solution)/shard_map/all_to_all | solution.py:896
  115.4 29.5 %shard_map.369 = (bf16[8,144,256]{2,1,0:T(8,128)(2,1)S(1)}, bf16[8,144,256]{2,1,0:T(8,128)(2,1)}) custom-call(s32[6]{0:T(128)S(1)} %reshape.329.bounds.target_bounds, s32[6]{0:T(128)S(1)} %reshape.333.source_bounds, s32[2]{0:T(128)S(1)} %pad_add_fusion.1.place, bf16[8,128,256]{2,1,0:T(8,128)(2,1)S(1)} %copy-done.35, ...), custom_call_target="tpu_custom_call" | custom-call | flops 3221225472 | bytes 6291456 | tf_op jit(solution)/shard_map/pallas_call | solution.py:319
  149.7 20.9 %all_to_all.52 = bf16[8,144,256]{2,1,0:T(8,128)(2,1)S(1)} all-to-all(bf16[8,144,256]{2,1,0:T(8,128)(2,1)S(1)} %fusion.32), channel_id=1, replica_groups={{0,4,8,12,16,20,24,28},{2,6,10,14,18,22,26,30},{1,5,9,13,17,21,25,29},{..., dimensions={0} | all-to-all | bytes 1179648 | tf_op jit(solution)/shard_map/all_to_all | solution.py:896
  173.6 10.9 %collective-permute-done.4 = bf16[256,1024]{1,0:T(8,128)(2,1)S(1)} collective-permute-done((bf16[256,1024]{1,0:T(8,128)(2,1)S(1)}, bf16[256,1024]{1,0:T(8,128)(2,1)S(1)}, u32[]{:S(2)}, u32[]{:S(2)}) %collective-permute-start.4) | collective-permute-done | bytes 524320 | tf_op jit(solution)/shard_map/ppermute | solution.py:906
  194.5 9.3 %collective-permute-done.5 = bf16[256,1024]{1,0:T(8,128)(2,1)S(1)} collective-permute-done((bf16[256,1024]{1,0:T(8,128)(2,1)S(1)}, bf16[256,1024]{1,0:T(8,128)(2,1)S(1)}, u32[]{:S(2)}, u32[]{:S(2)}) %collective-permute-start.5) | collective-permute-done | bytes 524320 | tf_op jit(solution)/shard_map/ppermute | solution.py:906
  206.0 8.3 %fusion.28 = f32[256,1024]{1,0:T(8,128)} fusion(bf16[1024,2048]{1,0:T(8,128)(2,1)} %param.35, f32[256,2048]{1,0:T(8,128)} %copy-done.85, bf16[256,1024]{1,0:T(8,128)(2,1)S(1)} %fusion.67.third_ref, bf16[2048,1024]{1,0:T(8,128)(2,1)} %param.36), kind=kOutput, calls=%fused_computation.72 | convolution fusion | flops 2157969408 | bytes 12058624 | tf_op jit(solution)/shard_map/dot_general | solution.py:24
  218.9 9.4 %collective-permute-done.6 = bf16[256,1024]{1,0:T(8,128)(2,1)} collective-permute-done((bf16[256,1024]{1,0:T(8,128)(2,1)}, bf16[256,1024]{1,0:T(8,128)(2,1)}, u32[]{:S(2)}, u32[]{:S(2)}) %collective-permute-start.6) | collective-permute-done | bytes 524320 | tf_op jit(solution)/shard_map/ppermute | solution.py:906
  228.3 4.7 multiply_reduce_fusion
  235.3 20.3 %all_to_all.53.own_g = bf16[8,144,256]{2,1,0:T(8,128)(2,1)S(1)} all-to-all(bf16[8,144,256]{2,1,0:T(8,128)(2,1)S(1)} %bitcast.221), channel_id=1, replica_groups={{0,4,8,12,16,20,24,28},{2,6,10,14,18,22,26,30},{1,5,9,13,17,21,25,29},{..., dimensions={0} | all-to-all | bytes 1179648 | tf_op jit(solution)/shard_map/all_to_all | solution.py:896
  257.6 32.8 %shard_map.371 = (bf16[8,128,256]{2,1,0:T(8,128)(2,1)S(1)}, bf16[8,128,256]{2,1,0:T(8,128)(2,1)S(1)}, bf16[4,2,768,128]{3,2,1,0:T(8,128)(2,1)S(1)}) custom-call(s32[6]{0:T(128)S(1)} %reshape.329.bounds.target_bounds, s32[6]{0:T(128)S(1)} %reshape.333.source_bounds, s32[2]{0:T(128)S(1)} %pad_add_fusion.1.place, bf16[8,128,256]{2,1,0:T(8,128)(2,1)S(1)} %copy-done.36, ...), custom_call_target="tpu_custom_call" | custom-call | flops 8053063680 | bytes 8388608 | tf_op jit(solution)/shard_map/pallas_call | solution.py:342
  294.6 17.9 %all_to_all.54 = bf16[8,128,256]{2,1,0:T(8,128)(2,1)S(1)} all-to-all(bf16[8,128,256]{2,1,0:T(8,128)(2,1)S(1)} %add_convert_fusion.1), channel_id=1, replica_groups={{0,4,8,12,16,20,24,28},{2,6,10,14,18,22,26,30},{1,5,9,13,17,21,25,29},{..., dimensions={0} | all-to-all | bytes 1048576 | tf_op jit(solution)/shard_map/all_to_all | solution.py:896
  318.7 11.1 %collective-permute-done.9 = bf16[256,1024]{1,0:T(8,128)(2,1)S(1)} collective-permute-done((bf16[256,1024]{1,0:T(8,128)(2,1)S(1)}, bf16[256,1024]{1,0:T(8,128)(2,1)S(1)}, u32[]{:S(2)}, u32[]{:S(2)}) %collective-permute-start.9) | collective-permute-done | bytes 524320 | tf_op jit(solution)/shard_map/ppermute | solution.py:906
  337.0 4.8 all-to-all-start.7
  350.3 7.2 %shard_map.372 = bf16[1024,3072]{1,0:T(8,128)(2,1)} custom-call(bf16[256,1024]{1,0:T(8,128)(2,1)S(1)} %copy-done.7, bf16[512,256]{1,0:T(8,128)(2,1)S(1)} %bitcast.213, bf16[256,1024]{1,0:T(8,128)(2,1)S(1)} %get-tuple-element.135.first_ref, bf16[512,256]{1,0:T(8,128)(2,1)S(1)} %bitcast.216, bf16[256,1024]{1,0:T(8,128)(2,1)S(1)} %copy-done.20, ...), custom_call_target="tpu_custom_call" | custom-call | flops 2684354560 | bytes 8388608 | tf_op jit(solution)/shard_map/pallas_call | solution.py:615
  358.6 12.5 %shard_map.373 = (bf16[8,128,128]{2,1,0:T(8,128)(2,1)S(1)}, bf16[8,2,128,128]{3,2,1,0:T(8,128)(2,1)S(1)}, bf16[8,2,128,128]{3,2,1,0:T(8,128)(2,1)S(1)}) custom-call(s32[6]{0:T(128)S(1)} %reshape.329.bounds.target_bounds, s32[2]{0:T(128)S(1)} %pad_add_fusion.place, bf16[8,128,128]{2,1,0:T(8,128)(2,1)S(1)} %copy-done.38, bf16[8,128,128]{2,1,0:T(8,128)(2,1)S(1)} %copy-done.40, ...), custom_call_target="tpu_custom_call" | custom-call | flops 3221225472 | bytes 6291456 | tf_op jit(solution)/shard_map/pallas_call | solution.py:579
  378.6 31.6 %all-to-all-done.9.back_ref = bf16[8,3,128,128]{3,2,1,0:T(8,128)(2,1)S(1)} async-done(((bf16[8,3,128,128]{3,2,1,0:T(8,128)(2,1)}), bf16[8,3,128,128]{3,2,1,0:T(8,128)(2,1)S(1)}, u32[]{:S(2)}, u32[]{:S(2)}) %all-to-all-start.9) | async-done | bytes 786464 | tf_op jit(solution)/shard_map/all_to_all | solution.py:896
  429.8 6.1 %collective-permute-done.27 = f32[6,1024]{1,0:T(8,128)S(1)} collective-permute-done((f32[6,1024]{1,0:T(8,128)S(1)}, f32[6,1024]{1,0:T(8,128)S(1)}, u32[]{:S(2)}, u32[]{:S(2)}) %collective-permute-start.27) | collective-permute-done | bytes 24608 | tf_op jit(solution)/shard_map/ppermute | solution.py:1128
  443.8 12.8 %collective-permute-done.12 = bf16[768,1024]{1,0:T(8,128)(2,1)} collective-permute-done((bf16[768,1024]{1,0:T(8,128)(2,1)}, bf16[768,1024]{1,0:T(8,128)(2,1)}, u32[]{:S(2)}, u32[]{:S(2)}) %collective-permute-start.12) | collective-permute-done | bytes 1572896 | tf_op jit(solution)/shard_map/ppermute | solution.py:911
  473.2 6.0 %collective-permute-done.20 = bf16[64,512]{1,0:T(8,128)(2,1)S(1)} collective-permute-done((bf16[64,512]{1,0:T(8,128)(2,1)S(1)}, bf16[64,512]{1,0:T(8,128)(2,1)S(1)}, u32[]{:S(2)}, u32[]{:S(2)}) %collective-permute-start.20) | collective-permute-done | bytes 65568 | tf_op jit(solution)/shard_map/ppermute | solution.py:1118
  (352 shorter events, 158.1 us)
Async XLA Ops:
  13.9 27.5 %all-to-all-start = ((bf16[8,3,128,128]{3,2,1,0:T(8,128)(2,1)}), bf16[8,3,128,128]{3,2,1,0:T(8,128)(2,1)S(1)}, u32[]{:S(2)}, u32[]{:S(2)}) async-start(bf16[8,3,128,128]{3,2,1,0:T(8,128)(2,1)} %shard_map.366), calls=%async_computation | async-start | bytes 1572864 | tf_op jit(solution)/shard_map/all_to_all | solution.py:896
  42.2 21.9 %all-to-all-start.1 = ((bf16[4,2,768,128]{3,2,1,0:T(8,128)(2,1)}), bf16[4,2,768,128]{3,2,1,0:T(8,128)(2,1)S(1)}, u32[]{:S(2)}, u32[]{:S(2)}) async-start(bf16[4,2,768,128]{3,2,1,0:T(8,128)(2,1)} %copy-done.28), calls=%async_computation.1 | async-start | bytes 3145728 | tf_op jit(solution)/shard_map/all_to_all | solution.py:901
  78.9 12.0 %collective-permute-start.1 = (bf16[256,1024]{1,0:T(8,128)(2,1)S(1)}, bf16[256,1024]{1,0:T(8,128)(2,1)S(1)}, u32[]{:S(2)}, u32[]{:S(2)}) collective-permute-start(bf16[256,1024]{1,0:T(8,128)(2,1)S(1)} %get-tuple-element.183), channel_id=1, source_target_pairs={{0,1},{1,0},{2,3},{3,2},{4,5},{5,4},{6,7},{7,6},{8,9},{9,8},{10,11... | collective-permute-start | bytes 1572872 | tf_op jit(solution)/shard_map/ppermute | solution.py:906
  172.1 12.4 %collective-permute-start.4 = (bf16[256,1024]{1,0:T(8,128)(2,1)S(1)}, bf16[256,1024]{1,0:T(8,128)(2,1)S(1)}, u32[]{:S(2)}, u32[]{:S(2)}) collective-permute-start(bf16[256,1024]{1,0:T(8,128)(2,1)S(1)} %get-tuple-element.185), channel_id=1, source_target_pairs={{0,1},{1,0},{2,3},{3,2},{4,5},{5,4},{6,7},{7,6},{8,9},{9,8},{10,11... | collective-permute-start | bytes 1572872 | tf_op jit(solution)/shard_map/ppermute | solution.py:906
  192.2 11.6 %collective-permute-start.5 = (bf16[256,1024]{1,0:T(8,128)(2,1)S(1)}, bf16[256,1024]{1,0:T(8,128)(2,1)S(1)}, u32[]{:S(2)}, u32[]{:S(2)}) collective-permute-start(bf16[256,1024]{1,0:T(8,128)(2,1)S(1)} %get-tuple-element.189), channel_id=1, source_target_pairs={{0,1},{1,0},{2,3},{3,2},{4,5},{5,4},{6,7},{7,6},{8,9},{9,8},{10,11... | collective-permute-start | bytes 1572872 | tf_op jit(solution)/shard_map/ppermute | solution.py:906
  217.4 10.9 %collective-permute-start.6 = (bf16[256,1024]{1,0:T(8,128)(2,1)}, bf16[256,1024]{1,0:T(8,128)(2,1)}, u32[]{:S(2)}, u32[]{:S(2)}) collective-permute-start(bf16[256,1024]{1,0:T(8,128)(2,1)} %get-tuple-element.191), channel_id=1, source_target_pairs={{0,1},{1,0},{2,3},{3,2},{4,5},{5,4},{6,7},{7,6},{8,9},{9,8},{10,11... | collective-permute-start | bytes 1572872 | tf_op jit(solution)/shard_map/ppermute | solution.py:906
  312.5 24.5 %all-to-all-start.8 = ((bf16[4,2,768,128]{3,2,1,0:T(8,128)(2,1)}), bf16[4,2,768,128]{3,2,1,0:T(8,128)(2,1)S(1)}, u32[]{:S(2)}, u32[]{:S(2)}) async-start(bf16[4,2,768,128]{3,2,1,0:T(8,128)(2,1)} %copy-done.29), calls=%async_computation.8 | async-start | bytes 3145728 | tf_op jit(solution)/shard_map/all_to_all | solution.py:901
  317.1 12.7 %collective-permute-start.9 = (bf16[256,1024]{1,0:T(8,128)(2,1)S(1)}, bf16[256,1024]{1,0:T(8,128)(2,1)S(1)}, u32[]{:S(2)}, u32[]{:S(2)}) collective-permute-start(bf16[256,1024]{1,0:T(8,128)(2,1)S(1)} %get-tuple-element.193), channel_id=1, source_target_pairs={{0,1},{1,0},{2,3},{3,2},{4,5},{5,4},{6,7},{7,6},{8,9},{9,8},{10,11... | collective-permute-start | bytes 1572872 | tf_op jit(solution)/shard_map/ppermute | solution.py:906
  337.0 20.4 %all-to-all-start.7 = ((bf16[8,128,128]{2,1,0:T(8,128)(2,1)}), bf16[8,128,128]{2,1,0:T(8,128)(2,1)}, u32[]{:S(2)}, u32[]{:S(2)}) async-start(bf16[8,128,128]{2,1,0:T(8,128)(2,1)} %bitcast.229), calls=%async_computation.7 | async-start | bytes 524288 | tf_op jit(solution)/shard_map/all_to_all | solution.py:896
  341.8 126.6 %reduce-scatter.2.cloned.1.call-start = ((), (), s32[]{:S(2)}) async-start(), calls=%async_computation.11 | async-start | bytes 6684672 | tf_op jit(solution)/shard_map/reduce_scatter | solution.py:1087
  374.3 35.9 %all-to-all-start.9 = ((bf16[8,3,128,128]{3,2,1,0:T(8,128)(2,1)}), bf16[8,3,128,128]{3,2,1,0:T(8,128)(2,1)S(1)}, u32[]{:S(2)}, u32[]{:S(2)}) async-start(bf16[8,3,128,128]{3,2,1,0:T(8,128)(2,1)} %pad_maximum_fusion.1), calls=%async_computation.9 | async-start | bytes 1572864 | tf_op jit(solution)/shard_map/all_to_all | solution.py:896
  414.9 26.8 %collective-permute-start.13 = (bf16[2,2,2,64,1536]{4,3,0,2,1:T(8,128)(2,1)}, bf16[2,2,2,64,1536]{4,3,0,2,1:T(8,128)(2,1)}, u32[]{:S(2)}, u32[]{:S(2)}) collective-permute-start(bf16[2,2,2,64,1536]{4,3,0,2,1:T(8,128)(2,1)} %bitcast.205), channel_id=1, source_target_pairs={{0,2},{2,0},{4,6},{6,4},{8,10},{10,8},{12,14},{14,12},{16,18},{18,... | collective-permute-start | bytes 4718600 | tf_op jit(solution)/shard_map/ppermute | solution.py:1096
  419.0 37.6 %collective-permute-start.12 = (bf16[768,1024]{1,0:T(8,128)(2,1)}, bf16[768,1024]{1,0:T(8,128)(2,1)}, u32[]{:S(2)}, u32[]{:S(2)}) collective-permute-start(bf16[768,1024]{1,0:T(8,128)(2,1)} %shard_map.375), channel_id=1, source_target_pairs={{0,1},{1,0},{2,3},{3,2},{4,5},{5,4},{6,7},{7,6},{8,9},{9,8},{10,11... | collective-permute-start | bytes 4718600 | tf_op jit(solution)/shard_map/ppermute | solution.py:911
  429.7 6.3 %collective-permute-start.27 = (f32[6,1024]{1,0:T(8,128)S(1)}, f32[6,1024]{1,0:T(8,128)S(1)}, u32[]{:S(2)}, u32[]{:S(2)}) collective-permute-start(f32[6,1024]{1,0:T(8,128)S(1)} %add.491), channel_id=1, source_target_pairs={{0,16},{2,18},{4,20},{6,22},{8,24},{10,26},{12,28},{14,30},{16,0},... | collective-permute-start | bytes 73736 | tf_op jit(solution)/shard_map/ppermute | solution.py:1128
  441.2 25.2 %collective-permute-start.11 = (bf16[256,1024]{1,0:T(8,128)(2,1)S(1)}, bf16[256,1024]{1,0:T(8,128)(2,1)S(1)}, u32[]{:S(2)}, u32[]{:S(2)}) collective-permute-start(bf16[256,1024]{1,0:T(8,128)(2,1)S(1)} %shard_map.374), channel_id=1, source_target_pairs={{0,1},{1,0},{2,3},{3,2},{4,5},{5,4},{6,7},{7,6},{8,9},{9,8},{10,11... | collective-permute-start | bytes 1572872 | tf_op jit(solution)/shard_map/ppermute | solution.py:911
  443.3 17.5 %collective-permute-start.14 = (bf16[2,2,64,768]{3,2,1,0:T(8,128)(2,1)S(1)}, bf16[2,2,64,768]{3,2,1,0:T(8,128)(2,1)S(1)}, u32[]{:S(2)}, u32[]{:S(2)}) collective-permute-start(bf16[2,2,64,768]{3,2,1,0:T(8,128)(2,1)S(1)} %fusion.33), channel_id=1, source_target_pairs={{0,4},{2,6},{4,0},{6,2},{8,12},{10,14},{12,8},{14,10},{16,20},{18,... | collective-permute-start | bytes 1179656 | tf_op jit(solution)/shard_map/ppermute | solution.py:1096
  443.8 17.2 %collective-permute-start.17 = (bf16[2,2,64,768]{3,2,1,0:T(8,128)(2,1)S(1)}, bf16[2,2,64,768]{3,2,1,0:T(8,128)(2,1)S(1)}, u32[]{:S(2)}, u32[]{:S(2)}) collective-permute-start(bf16[2,2,64,768]{3,2,1,0:T(8,128)(2,1)S(1)} %copy.101), channel_id=1, source_target_pairs={{0,8},{2,10},{4,12},{6,14},{8,0},{10,2},{12,4},{14,6},{16,24},{18,... | collective-permute-start | bytes 1179656 | tf_op jit(solution)/shard_map/ppermute | solution.py:1096
  460.9 6.7 %collective-permute-start.15 = (bf16[2,64,768]{2,1,0:T(8,128)(2,1)S(1)}, bf16[2,64,768]{2,1,0:T(8,128)(2,1)S(1)}, u32[]{:S(2)}, u32[]{:S(2)}) collective-permute-start(bf16[2,64,768]{2,1,0:T(8,128)(2,1)S(1)} %fusion.36), channel_id=1, source_target_pairs={{0,8},{2,10},{4,12},{6,14},{8,0},{10,2},{12,4},{14,6},{16,24},{18,... | collective-permute-start | bytes 589832 | tf_op jit(solution)/shard_map/ppermute | solution.py:1096
  461.8 10.4 %collective-permute-start.18 = (bf16[2,64,768]{2,1,0:T(8,128)(2,1)}, bf16[2,64,768]{2,1,0:T(8,128)(2,1)}, u32[]{:S(2)}, u32[]{:S(2)}) collective-permute-start(bf16[2,64,768]{2,1,0:T(8,128)(2,1)} %fusion.35), channel_id=1, source_target_pairs={{0,4},{2,6},{4,0},{6,2},{8,12},{10,14},{12,8},{14,10},{16,20},{18,... | collective-permute-start | bytes 589832 | tf_op jit(solution)/shard_map/ppermute | solution.py:1096
  468.4 11.8 %collective-permute-start.16 = (bf16[64,768]{1,0:T(8,128)(2,1)}, bf16[64,768]{1,0:T(8,128)(2,1)S(1)}, u32[]{:S(2)}, u32[]{:S(2)}) collective-permute-start(bf16[64,768]{1,0:T(8,128)(2,1)} %fusion.47), channel_id=1, source_target_pairs={{0,16},{2,18},{4,20},{6,22},{8,24},{10,26},{12,28},{14,30},{16,0},... | collective-permute-start | bytes 294920 | tf_op jit(solution)/shard_map/ppermute | solution.py:1096
  469.2 10.0 %collective-permute-start.20 = (bf16[64,512]{1,0:T(8,128)(2,1)S(1)}, bf16[64,512]{1,0:T(8,128)(2,1)S(1)}, u32[]{:S(2)}, u32[]{:S(2)}) collective-permute-start(bf16[64,512]{1,0:T(8,128)(2,1)S(1)} %slice.118), channel_id=1, source_target_pairs={{0,16},{2,18},{4,20},{6,22},{8,24},{10,26},{12,28},{14,30},{16,0},... | collective-permute-start | bytes 196616 | tf_op jit(solution)/shard_map/ppermute | solution.py:1118
  473.1 14.1 %collective-permute-start.19 = (bf16[64,768]{1,0:T(8,128)(2,1)S(1)}, bf16[64,768]{1,0:T(8,128)(2,1)S(1)}, u32[]{:S(2)}, u32[]{:S(2)}) collective-permute-start(bf16[64,768]{1,0:T(8,128)(2,1)S(1)} %fusion.44), channel_id=1, source_target_pairs={{0,16},{2,18},{4,20},{6,22},{8,24},{10,26},{12,28},{14,30},{16,0},... | collective-permute-start | bytes 294920 | tf_op jit(solution)/shard_map/ppermute | solution.py:1096
  480.1 5.0 collective-permute-start.21
  485.2 6.6 %collective-permute-start.22 = (bf16[2,2,64,512]{3,2,0,1:T(8,128)(2,1)S(1)}, bf16[2,2,64,512]{3,2,0,1:T(8,128)(2,1)S(1)}, u32[]{:S(2)}, u32[]{:S(2)}) collective-permute-start(bf16[2,2,64,512]{3,2,0,1:T(8,128)(2,1)S(1)} %pad_maximum_fusion.3), channel_id=1, source_target_pairs={{0,4},{2,6},{4,0},{6,2},{8,12},{10,14},{12,8},{14,10},{16,20},{18,... | collective-permute-start | bytes 786440 | tf_op jit(solution)/shard_map/ppermute | solution.py:1118
  (96 other events, 744.6 us)
Sparse Core Ops, SparseCore 0:
  357.6 89.6 reduce-scatter.1
